TPU v7x, 32 devices: a whole 2x2x4 slice. The times are simulated.
32 devices in a mesh: seq: 4 (over y, x), head: 8 (over z, core).
Axes of the slice: x: 2, y: 2, z: 4, core: 2. Of those that a mesh axis runs over, the one named last changes fastest.
Arguments:
- x_heads: bfloat16 [2, 1024, 16384], P(None, 'seq', 'head'), may hold values from -6 to 6
- gate_z: bfloat16 [2, 1024, 16384], P(None, 'seq', 'head'), may hold values from -6 to 6
- b_proj: bfloat16 [2, 1024, 128], P(None, 'seq'), may hold values from -0.59765625 to 0.59765625
- c_proj: bfloat16 [2, 1024, 128], P(None, 'seq'), may hold values from -6 to 6
- dt_raw: float32 [2, 1024, 256], P(None, 'seq', 'head'), may hold values from -3 to 3
- dt_bias: float32 [2, 256], P(None, 'head'), may hold values from -1 to 0.5
- decay_rate: float32 [2, 256], P(None, 'head'), may hold values from 0 to 1, as said below
- skip_d: float32 [2, 256], P(None, 'head'), may hold values from 0.5 to 1.5
- norm_gain: float32 [2, 16384], P(None, 'head'), may hold values from 0.5 to 1.5
- w_out: bfloat16 [2, 16384, 8192], P(None, 'head', 'seq'), may hold values from -0.046875 to 0.046875
- seg_ids: int32 [1024], P('seq'), may hold values from 0 to 2, never falling along the last dimension, each value on 1 to 512 neighbouring positions
Outputs:
- mixed: bfloat16 [2, 1024, 8192], P(None, 'head', 'seq')
Inputs may be any that keep to these rules, and one draw needn't show every extreme that they name: `decay_rate`: Positive. `seg_ids`: document numbers start at 0, never fall along the sequence and take every value; one document has exactly 512 tokens.
All inputs are finite; a program needn't handle non-finite values.
Results may differ from a plain program's by a relative error of at most 0.019.
Values may be sent and summed in bfloat16 or wider, within the bound.
No kernel may reach another device: no remote copies, remote signals or barrier semaphores. Data moves between devices by JAX's collectives and lax.ppermute only.
A program may use at most 128 MiB of HBM per device.

v0:
```python
import jax
import jax.numpy as jnp
from jax import lax
from jax.sharding import PartitionSpec as P

HEADS = 256
HEADDIM = 64
SPAN = 256


highest = lax.Precision.HIGHEST


def passed_along(block, axis, distance):
    devices = range(lax.axis_size(axis))
    route = [(i - distance, i) for i in devices if i - distance in devices]
    return lax.ppermute(block, axis, route)


def entering_2(value, axis, combine, identity):
    devices, position = (lax.axis_size(axis), lax.axis_index(axis))
    everything = jax.tree.map(
        lambda part, kind: lax.all_gather(part.astype(kind), axis),
        value,
        (jnp.bfloat16, jnp.bfloat16),
    )
    start = jax.tree.map(
        lambda part, zero: jnp.broadcast_to(jnp.asarray(zero, part.dtype), part.shape),
        value,
        identity,
    )

    def hop(k, before):
        reached = k < position
        new = combine(
            before, jax.tree.map(lambda part, own: part[k].astype(own.dtype), everything, value)
        )
        return jax.tree.map(lambda a, b: jnp.where(reached, a, b), new, before)

    return lax.fori_loop(0, devices, hop, start)


def to_blocks(tensor, nblocks):
    shaped = tensor.reshape(
        (tensor.shape[0], nblocks, tensor.shape[1] // nblocks) + tensor.shape[2:]
    )
    return jnp.moveaxis(shaped, 1, 0)


def from_blocks(tensor):
    moved = jnp.moveaxis(tensor, 0, 1)
    return moved.reshape((moved.shape[0], moved.shape[1] * moved.shape[2]) + moved.shape[3:])


def span_state(carried, before, offset, anchor, pieces):
    x_block, b_block, c_block, step_block, decay_block, seg_block = pieces
    running = jnp.cumsum(decay_block, axis=1)
    total = running[:, -1, :]
    kept = (seg_block == before).astype(jnp.float32)
    same_last = (seg_block == seg_block[-1]).astype(jnp.float32)
    tail_w = jnp.exp(total[:, None, :] - running) * same_last[None, :, None] * step_block
    fresh = jnp.einsum("mjh,mjhp,mjn->mhpn", tail_w, x_block, b_block, precision=highest)
    new_state = (jnp.exp(total) * kept[-1])[:, :, None, None] * carried + fresh
    factor = (
        jnp.exp(offset[:, None, :] + running)
        * (seg_block == anchor).astype(jnp.float32)[None, :, None]
    )
    return (new_state, factor, total)


def span_output(carried, before, pieces):
    x_block, b_block, c_block, step_block, decay_block, seg_block = pieces
    running = jnp.cumsum(decay_block, axis=1)
    kept = (seg_block == before).astype(jnp.float32)
    entry_w = jnp.exp(running) * kept[None, :, None]
    places = jnp.arange(seg_block.shape[0], dtype=jnp.int32)
    lower_mask = (places[:, None] >= places[None, :]) & (seg_block[:, None] == seg_block[None, :])
    run_t = jnp.transpose(running, (0, 2, 1))
    spread = run_t[:, :, :, None] - run_t[:, :, None, :]
    mixing = jnp.exp(jnp.minimum(spread, 0.0)) * lower_mask.astype(jnp.float32)
    products = jnp.einsum("min,mjn->mij", c_block, b_block, precision=highest)
    weights = mixing * products[:, None] * jnp.transpose(step_block, (0, 2, 1))[:, :, None, :]
    inside = jnp.einsum("mhij,mjhp->mihp", weights, x_block, precision=highest)
    entering = jnp.einsum("min,mhpn->mihp", c_block, carried, precision=highest)
    return inside + entry_w[..., None] * entering


def combine_pairs(earlier, later):
    return (earlier[0] * later[0], later[1] + later[0][:, :, None, None] * earlier[1])


def local(
    x_heads, gate_z, b_proj, c_proj, dt_raw, dt_bias, decay_rate, skip_d, norm_gain, w_out, seg_ids
):
    rows = x_heads.shape[1]
    local_heads = dt_raw.shape[2]
    head_size = x_heads.shape[2] // local_heads
    block = min(SPAN, rows)
    nblocks = rows // block
    step_size = jax.nn.softplus(dt_raw + dt_bias[:, None, :])
    log_decay = -decay_rate[:, None, :] * step_size
    x_float = x_heads.astype(jnp.float32).reshape(2, rows, local_heads, head_size)
    b_float = b_proj.astype(jnp.float32)
    c_float = c_proj.astype(jnp.float32)
    pieces = (
        to_blocks(x_float, nblocks),
        to_blocks(b_float, nblocks),
        to_blocks(c_float, nblocks),
        to_blocks(step_size, nblocks),
        to_blocks(log_decay, nblocks),
        seg_ids.reshape(nblocks, block),
    )
    anchor = passed_along(seg_ids[rows - 1 :], "seq", 1)[0]
    offset_zero = jnp.zeros((2, local_heads), jnp.float32)
    empty = jnp.zeros((2, local_heads, head_size, b_proj.shape[2]), jnp.float32)

    def joint_turn(carry, piece_set):
        carried, before, offset = carry
        output = span_output(carried, before, piece_set)
        new_state, factor, total = span_state(carried, before, offset, anchor, piece_set)
        return ((new_state, piece_set[5][-1], offset + total), (output, factor))

    ends, (outputs, factors) = lax.scan(joint_turn, (empty, anchor, offset_zero), pieces)
    local_state = ends[0]
    factor_all = from_blocks(factors)
    decay_dev = factor_all[:, -1, :]
    decay_unused, state_in = entering_2(
        (decay_dev, local_state),
        "seq",
        combine_pairs,
        (jnp.ones_like(decay_dev), jnp.zeros_like(local_state)),
    )
    entering = jnp.einsum("mtn,mhpn->mthp", c_float, state_in, precision=highest)
    ssd_out = (
        from_blocks(outputs) + factor_all[..., None] * entering + skip_d[:, None, :, None] * x_float
    )
    gated = ssd_out.reshape(2, rows, local_heads * head_size) * jax.nn.silu(
        gate_z.astype(jnp.float32)
    )
    square_sum = lax.psum(jnp.sum(gated * gated, axis=2), "head")
    mean_square = square_sum / (HEADS * HEADDIM)
    normed = (gated * lax.rsqrt(mean_square + 1e-05)[:, :, None] * norm_gain[:, None, :]).astype(
        jnp.bfloat16
    )
    partial_terms = jnp.einsum(
        "mtk,mkd->mtd",
        lax.all_gather(normed, "seq", axis=1, tiled=True),
        w_out,
        preferred_element_type=jnp.float32,
    )
    summed = lax.psum_scatter(
        partial_terms.astype(jnp.bfloat16), "head", scatter_dimension=1, tiled=True
    )
    return summed


def solution(mesh):
    placed = (
        P(None, "seq", "head"),
        P(None, "seq", "head"),
        P(None, "seq", None),
        P(None, "seq", None),
        P(None, "seq", "head"),
        P(None, "head"),
        P(None, "head"),
        P(None, "head"),
        P(None, "head"),
        P(None, "head", "seq"),
        P("seq"),
    )
    return jax.shard_map(
        local, mesh=mesh, in_specs=placed, out_specs=P(None, "head", "seq"), check_vma=False
    )
```

profile of v0, /device:TPU:0, one launch (start us, length us, event | category | flops | bytes accessed | tf_op | source)
XLA Modules:
  0.0 338.4 jit_solution(8063180244486173514)
XLA Ops:
  6.5 0.0 copy-start
  6.5 0.0 copy-start.9
  6.5 0.0 copy-start.10
  6.5 0.0 copy-start.6
  6.5 0.0 copy-start.7
  6.5 0.0 all-gather.7.cloned.1.call-start
  6.6 1.4 slice.26
  8.0 5.3 %collective-permute-start = (s32[1]{0:T(128)}, s32[1]{0:T(128)}, u32[]{:S(2)}, u32[]{:S(2)}) collective-permute-start(s32[1]{0:T(128)} %slice.26), channel_id=1, source_target_pairs={{0,8},{8,16},{16,24},{1,9},{9,17},{17,25},{2,10},{10,18},{18,26},{... | collective-permute-start | bytes 20 | tf_op jit(solution)/shard_map/ppermute | solution.py:17
  13.3 0.7 neg.12
  14.0 0.9 copy_bitcast_fusion.1
  14.9 1.2 reduce-window.6
  16.1 0.2 slice_reduce_fusion
  16.3 0.1 copy_bitcast_fusion
  16.4 0.2 slice_reduce_fusion.1
  16.6 2.9 copy.21
  19.4 0.0 copy-start.4
  19.4 0.0 collective-permute-done
  19.5 0.0 copy-done.9
  19.5 1.3 compare_convert_fusion.1
  20.7 0.6 slice.28
  21.3 0.7 multiply_multiply_fusion.1
  22.0 0.0 copy-done.10
  22.0 0.0 copy-done.6
  22.0 0.1 fusion.35
  22.1 0.0 copy-done.7
  22.1 3.2 add_convert_fusion
  25.3 0.0 all-gather.7.cloned.1.call-update
  25.4 0.0 all-gather.5.cloned.1.call-start
  25.4 0.0 copy-done.4
  25.4 0.1 fusion.28
  25.5 0.0 copy-done
  25.6 0.2 fusion.37
  25.8 3.7 %fusion.25 = f32[2,32,64,256]{3,2,1,0:T(8,128)} fusion(bf16[2,256,128]{2,1,0:T(8,128)(2,1)S(1)} %copy-done), kind=kOutput, calls=%fused_computation.35 | convolution fusion | flops 1610612736 | bytes 4325376 | tf_op jit(solution)/shard_map/while/body/eval_jaxpr/min,mhpn->mihp/dot_general | solution.py:84
  29.5 0.1 slice.37
  29.6 0.1 copy.22
  29.7 7.8 %all-gather.1 = bf16[8,1,32]{2,1,0:T(2,128)(2,1)S(1)} all-gather(bf16[2,1,32]{2,1,0:T(2,128)(2,1)S(1)} %copy.22), channel_id=3, replica_groups=mesh['seq'=4,'head'=8] {'seq'}, dimensions={0}, use_global_device_ids=true | all-gather | bytes 640 | tf_op jit(solution)/shard_map/all_gather | solution.py:23
  37.4 40.6 %all-gather.7.cloned.1.call-done = bf16[8,32,64,128]{3,2,1,0:T(8,128)(2,1)} async-done(((bf16[2,32,64,128]{3,2,1,0:T(8,128)(2,1)}), bf16[8,32,64,128]{3,2,1,0:T(8,128)(2,1)}) %all-gather.7.cloned.1.call-update) | async-done | bytes 4194320 | tf_op jit(solution)/shard_map/all_gather | solution.py:23
  78.1 7.2 %while.9 = (s32[]{:T(128)}, f32[2,32,64,128]{3,2,1,0:T(8,128)S(1)}, s32[]{:T(128)}, bf16[4,2,32,64,128]{4,3,2,1,0:T(8,128)(2,1)}, bf16[4,2,32]{2,1,0:T(2,128)(2,1)S(1)}, /*index=5*/s32[]{:T(128)}, s32[]{:T(128)}) while((s32[]{:T(128)}, f32[2,32,64,128]{3,2,1,0:T(8,128)S(1)}, s32[]{:T(128)}, bf16[4,2,32,64,128]{4,3,2,1,0:T(8,128)(2,1)}, ...), condition=%wide.region_3.4_spmd.clone, body=%wide.region_2.3_spmd.clone.sunk | while | flops 2621508 | bytes 5243633 | solution.py:40
  78.1 1.8 fusion.45
  79.9 1.8 fusion.45
  81.7 1.8 fusion.45
  83.5 1.8 fusion.45
  85.3 0.0 copy-start.3
  85.3 0.0 copy-start.5
  85.3 0.0 copy-start.11
  85.3 1.8 fusion.30
  87.1 0.4 copy-done.3
  87.5 0.7 copy-done.5
  88.2 0.0 copy-done.11
  88.2 14.2 %fusion.15 = f32[2,256,32,64]{1,3,2,0:T(8,128)} fusion(bf16[2,256,32,64]{1,3,2,0:T(8,128)(2,1)S(1)} %bitcast.76, f32[2,32,64,256]{3,2,1,0:T(8,128)S(1)} %fusion.30, f32[2,32,64,256]{3,2,1,0:T(8,128)S(1)} %copy-done.3, f32[2,32,256]{2,1,0:T(8,128)S(1)} %get-tuple-element.167, f32[2,256,256]{2,1,0:T(8,128)S(1)} %fusion.37, f32[256,256]{1,0:T(8,128)S(1)} %fusion.28, ...), kind=kOutput, calls=%fused_computation.22 | convolution fusion | flops 3249537024 | bytes 15663360 | tf_op jit(solution)/shard_map/while/body/eval_jaxpr/mhij,mjhp->mihp/dot_general | solution.py:83
  102.3 0.0 copy-start.2
  102.4 5.6 %copy.23 = f32[2,256,2048]{2,1,0:T(8,128)} copy(f32[2,256,2048]{1,2,0:T(8,128)} %bitcast.74) | data formatting | bytes 8388608 | tf_op jit(solution)/shard_map/reshape | solution.py:137
  108.0 0.0 copy-done.2
  108.0 3.6 %multiply_reduce_fusion = f32[2,256]{1,0:T(2,128)S(1)} fusion(f32[2,256,2048]{2,1,0:T(8,128)} %copy.23, bf16[2,256,2048]{2,1,0:T(8,128)(2,1)S(1)} %copy-done.2), kind=kLoop, calls=%fused_computation.32 | loop fusion | flops 8388096 | bytes 6293504 | tf_op jit(solution)/shard_map/reduce_sum | solution.py:140
  111.5 16.3 %psum.7 = f32[2,256]{1,0:T(2,128)S(1)} all-reduce(f32[2,256]{1,0:T(2,128)S(1)} %multiply_reduce_fusion), channel_id=1, replica_groups=mesh['seq'=4,'head'=8] {'head'}, use_global_device_ids=true, to_apply=%region_5.6 | all-reduce | flops 512 | bytes 4096 | tf_op jit(solution)/shard_map/psum | solution.py:140
  127.9 0.0 copy-done.8
  127.9 5.2 %multiply_convert_fusion = bf16[2,256,2048]{2,1,0:T(8,128)(2,1)} fusion(f32[2,2048]{1,0:T(2,128)S(1)} %copy-done.8, f32[2,256]{1,0:T(2,128)S(1)} %add_rsqrt_fusion, f32[2,256,2048]{2,1,0:T(8,128)} %copy.23, bf16[2,256,2048]{2,1,0:T(8,128)(2,1)S(1)} %copy-done.2), kind=kLoop, calls=%fused_computation.31 | loop fusion | flops 9437184 | bytes 8407040 | tf_op jit(solution)/shard_map/convert_element_type | solution.py:142
  133.1 0.0 all-gather.5.cloned.1.call-update
  133.1 0.3 reduce-scatter.2.cloned.1.call-start
  133.4 84.7 %all-gather.5.cloned.1.call-done = bf16[2,1024,2048]{2,1,0:T(8,128)(2,1)} async-done(((bf16[2,256,2048]{2,1,0:T(8,128)(2,1)}), bf16[2,1024,2048]{2,1,0:T(8,128)(2,1)}) %all-gather.5.cloned.1.call-update) | async-done | bytes 8388624 | tf_op jit(solution)/shard_map/all_gather | solution.py:147
  218.1 23.9 %convolution_convert_fusion = bf16[2,1024,2048]{2,1,0:T(8,128)(2,1)} fusion(bf16[2,1024,2048]{2,1,0:T(8,128)(2,1)} %all-gather.5.cloned.1.call-done, bf16[2,2048,2048]{2,1,0:T(8,128)(2,1)} %param.22), kind=kOutput, calls=%fused_computation.16 | convolution fusion | flops 17184063488 | bytes 33554432 | tf_op jit(solution)/shard_map/mtk,mkd->mtd/dot_general | solution.py:145
  242.1 0.0 reduce-scatter.2.cloned.1.call-update
  242.1 89.8 %reduce-scatter.2.cloned.1.call-done = bf16[2,128,2048]{2,1,0:T(8,128)(2,1)} async-done(((bf16[2,1024,2048]{2,1,0:T(8,128)(2,1)}), bf16[2,128,2048]{2,1,0:T(8,128)(2,1)}) %reduce-scatter.2.cloned.1.call-update) | async-done | bytes 1048592 | tf_op jit(solution)/shard_map/reduce_scatter | solution.py:151
  331.9 0.0 copy-done.1
  (11 shorter events, 0.1 us)
Async XLA Ops:
  6.5 19.0 %copy-start = (bf16[2,256,128]{2,1,0:T(8,128)(2,1)S(1)}, bf16[2,256,128]{2,1,0:T(8,128)(2,1)}, u32[]{:S(2)}) copy-start(bf16[2,256,128]{2,1,0:T(8,128)(2,1)} %param.16) | copy-start | bytes 393220
  6.5 12.9 %copy-start.9 = (s32[256]{0:T(256)S(1)}, s32[256]{0:T(256)}, u32[]{:S(2)}) copy-start(s32[256]{0:T(256)} %param.23) | copy-start | bytes 3076
  6.5 15.4 %copy-start.10 = (f32[2,32]{1,0:T(2,128)S(1)}, f32[2,32]{1,0:T(2,128)}, u32[]{:S(2)}) copy-start(f32[2,32]{1,0:T(2,128)} %param.18) | copy-start | bytes 772
  6.5 15.4 %copy-start.6 = (f32[2,256,32]{1,2,0:T(8,128)S(1)}, f32[2,256,32]{1,2,0:T(8,128)}, u32[]{:S(2)}) copy-start(f32[2,256,32]{1,2,0:T(8,128)} %param.17) | copy-start | bytes 196612
  6.5 15.6 %copy-start.7 = (bf16[2,256,128]{2,1,0:T(8,128)(2,1)S(1)}, bf16[2,256,128]{2,1,0:T(8,128)(2,1)}, u32[]{:S(2)}) copy-start(bf16[2,256,128]{2,1,0:T(8,128)(2,1)} %param.15) | copy-start | bytes 393220
  6.5 71.5 %all-gather.7.cloned.1.call-start = ((), (), s32[]{:S(2)}) async-start(), calls=%async_computation.3 | async-start | bytes 5242880 | tf_op jit(solution)/shard_map/all_gather | solution.py:23
  8.0 11.5 %collective-permute-start = (s32[1]{0:T(128)}, s32[1]{0:T(128)}, u32[]{:S(2)}, u32[]{:S(2)}) collective-permute-start(s32[1]{0:T(128)} %slice.26), channel_id=1, source_target_pairs={{0,8},{8,16},{16,24},{1,9},{9,17},{17,25},{2,10},{10,18},{18,26},{... | collective-permute-start | bytes 20 | tf_op jit(solution)/shard_map/ppermute | solution.py:17
  19.4 6.0 %copy-start.4 = (bf16[2,256,2048]{1,2,0:T(8,128)(2,1)}, bf16[2,256,2048]{1,2,0:T(8,128)(2,1)S(1)}, u32[]{:S(2)}) copy-start(bf16[2,256,2048]{1,2,0:T(8,128)(2,1)S(1)} %copy.21) | copy-start | bytes 6291460
  25.4 192.8 %all-gather.5.cloned.1.call-start = ((), (), s32[]{:S(2)}) async-start(), calls=%async_computation.1 | async-start | bytes 10485760 | tf_op jit(solution)/shard_map/all_gather | solution.py:147
  85.3 2.2 copy-start.3
  85.3 2.9 copy-start.5
  85.3 2.9 copy-start.11
  102.3 5.6 %copy-start.2 = (bf16[2,256,2048]{2,1,0:T(8,128)(2,1)S(1)}, bf16[2,256,2048]{2,1,0:T(8,128)(2,1)}, u32[]{:S(2)}) copy-start(bf16[2,256,2048]{2,1,0:T(8,128)(2,1)} %param.14) | copy-start | bytes 6291460
  108.0 19.9 %copy-start.8 = (f32[2,2048]{1,0:T(2,128)S(1)}, f32[2,2048]{1,0:T(2,128)}, u32[]{:S(2)}) copy-start(f32[2,2048]{1,0:T(2,128)} %param.21) | copy-start | bytes 49156
  133.1 198.8 %reduce-scatter.2.cloned.1.call-start = ((), (), s32[]{:S(2)}) async-start(), calls=%async_computation.2 | async-start | bytes 9437184 | tf_op jit(solution)/shard_map/reduce_scatter | solution.py:151
  242.1 89.8 %copy-start.1 = (bf16[2,256,128]{2,1,0:T(8,128)(2,1)S(1)}, bf16[2,256,128]{2,1,0:T(8,128)(2,1)}, u32[]{:S(2)}) copy-start(bf16[2,256,128]{2,1,0:T(8,128)(2,1)} %param.16) | copy-start | bytes 393220
Sparse Core Ops, SparseCore 0:
  25.5 52.5 all-gather.6
  133.3 84.8 all-gather.4
  242.2 89.6 reduce-scatter.1
where the time goes:
time: 339 us; the launch traced here: 338 us
  waiting for transfers between devices  215 us (63%)
  matrix products  47.1 us (14%)
  blocking collectives  24.1 us (7%)
  other arithmetic  21 us (6%)
  between operations  13.3 us (4%)
  local copies, waits for them, and re-layouts  12 us (4%)
  starting transfers between devices  5.68 us (2%)
    reduce_scatter x1, waiting for transfers between devices, local(): lax.psum_scatter(partial_terms.astype(jnp.bfloat16), 'head', scatter_dime...  89.8 us
    all_gather x1, waiting for transfers between devices, local(): lax.all_gather(normed, 'seq', axis=1, tiled=True)  84.7 us
    all_gather x1, waiting for transfers between devices, entering_2(): lax.all_gather(part.astype(kind), axis)  40.6 us
    dot_general x1, matrix products, local(): jnp.einsum('mtk,mkd->mtd', lax.all_gather(normed, 'seq', axis=1, tiled=Tr...  23.9 us
    psum x1, blocking collectives, local(): square_sum = lax.psum(jnp.sum(gated * gated, axis=2), 'head')  16.3 us
    dot_general x1, matrix products, span_output(): inside = jnp.einsum('mhij,mjhp->mihp', weights, x_block, precision=highest)  14.2 us
    all_gather x1, blocking collectives, entering_2(): lax.all_gather(part.astype(kind), axis)  7.76 us
    select_n x4, other arithmetic, hop(): return jax.tree.map(lambda a, b: jnp.where(reached, a, b), new, before)  7.12 us
  transfers between devices with their start and end apart: 4, of which 3 were waited for; matrix products, arithmetic and copies ran while one was open for 3% of the time, Pallas kernels for 0%

commit v1 on v0

v1 whole, which is shorter than its diff:
```python
import functools
import jax
import jax.numpy as jnp
from jax import lax
from jax.experimental import pallas as pl
from jax.experimental.pallas import tpu as pltpu
from jax.sharding import PartitionSpec as P

F32, BF16 = jnp.float32, jnp.bfloat16
LANES = 128
EXTRA = 16
NEG = -1e30
EPS = 1e-05
PARAMS = pltpu.CompilerParams(vmem_limit_bytes=32 * 1024 * 1024)


def cost(flops, moved, trans=0):
    return pl.CostEstimate(flops=int(flops), bytes_accessed=int(moved), transcendentals=int(trans))


def dot(a, b):
    return jnp.dot(a, b, preferred_element_type=F32)


def lane_split(head_size, shape):
    return lax.broadcasted_iota(jnp.int32, shape, 1) // head_size


def spread(values, lane_head, first):
    shape = (values.shape[0], LANES)
    out = jnp.broadcast_to(values[:, first : first + 1], shape)
    for k in range(1, lane_head[1]):
        out = jnp.where(lane_head[0] == k, values[:, first + k : first + k + 1], out)
    return out


def lane_heads(head_size):
    return (lane_split(head_size, (1, LANES)), LANES // head_size)


def column(row):
    return jnp.broadcast_to(row, (LANES, row.shape[1])).T[:, :1]


def prep_kernel(model, head_size, x_ref, b_ref, raw_ref, bias_ref, rate_ref, seg_ref, msg_ref, run_ref, q_ref, step_ref):
    rows, channels = x_ref.shape[1:]
    heads = raw_ref.shape[2]
    state = b_ref.shape[2]
    step = jax.nn.softplus(raw_ref[0] + bias_ref[model : model + 1, :])
    log_decay = -rate_ref[model : model + 1, :] * step
    places = lax.broadcasted_iota(jnp.int32, (rows, rows), 0)
    others = lax.broadcasted_iota(jnp.int32, (rows, rows), 1)
    tri = (places >= others).astype(F32)
    run = jnp.dot(tri, log_decay, precision=lax.Precision.HIGHEST, preferred_element_type=F32)
    run_ref[...] = run
    step_ref[...] = step
    q = jnp.concatenate([run - jnp.log(step), jnp.zeros((rows, LANES - heads), F32)], axis=1)
    q_ref[...] = q.T[:heads]
    seg_row = seg_ref[...].astype(F32)
    seg_col = column(seg_row)
    last = seg_row[:, rows - 1 :]
    total = run[rows - 1 :, :]
    tail = jnp.exp(total - run) * step * (seg_col == last).astype(F32)
    etot = jnp.exp(total)
    b_t = b_ref[0].astype(F32).T.astype(BF16)
    lane_head = lane_heads(head_size)
    row_id = lax.broadcasted_iota(jnp.int32, (EXTRA, LANES), 0)
    for p in range(channels // LANES):
        cols = slice(p * LANES, (p + 1) * LANES)
        first = p * lane_head[1]
        xw = (x_ref[0, :, cols].astype(F32) * spread(tail, lane_head, first)).astype(BF16)
        msg_ref[:state, cols] = dot(b_t, xw).astype(BF16)
        decay = spread(etot, lane_head, first)
        high = decay.astype(BF16).astype(F32)
        extra = jnp.where(row_id == 0, high, jnp.where(row_id == 1, decay - high, jnp.where(row_id == 2, last, 0.0)))
        msg_ref[state:, cols] = extra.astype(BF16)


def prep(model, head_size, x, b, raw, bias, rate, seg_row):
    _, rows, channels = x.shape
    heads, state = raw.shape[2], b.shape[2]
    at = lambda i: (model, 0, 0)
    whole = lambda i: (0, 0)
    return pl.pallas_call(
        functools.partial(prep_kernel, model, head_size),
        name=f"prep_{model}",
        grid=(1,),
        in_specs=[
            pl.BlockSpec((1, rows, channels), at),
            pl.BlockSpec((1, rows, state), at),
            pl.BlockSpec((1, rows, heads), at),
            pl.BlockSpec(bias.shape, whole),
            pl.BlockSpec(rate.shape, whole),
            pl.BlockSpec(seg_row.shape, whole),
        ],
        out_specs=[
            pl.BlockSpec((state + EXTRA, channels), whole),
            pl.BlockSpec((rows, heads), whole),
            pl.BlockSpec((heads, rows), whole),
            pl.BlockSpec((rows, heads), whole),
        ],
        out_shape=[
            jax.ShapeDtypeStruct((state + EXTRA, channels), BF16),
            jax.ShapeDtypeStruct((rows, heads), F32),
            jax.ShapeDtypeStruct((heads, rows), F32),
            jax.ShapeDtypeStruct((rows, heads), F32),
        ],
        compiler_params=PARAMS,
        cost_estimate=cost(2 * rows * state * channels, 2 * rows * channels + 2 * state * channels),
    )(x, b, raw, bias, rate, seg_row)


def inside_kernel(model, head_size, x_ref, gate_ref, b_ref, c_ref, run_ref, q_ref, step_ref, skip_ref, seg_ref, yg_ref, fg_ref):
    rows, channels = x_ref.shape[1:]
    half = rows // 2
    lane_head = lane_heads(head_size)
    run, q = run_ref[...], q_ref[...]
    seg_row = seg_ref[...].astype(F32)
    seg_col = column(seg_row)
    products = lax.dot_general(c_ref[0], b_ref[0], (((1,), (1,)), ((), ())), preferred_element_type=F32)
    tri = lax.broadcasted_iota(jnp.int32, (half, half), 0) >= lax.broadcasted_iota(jnp.int32, (half, half), 1)
    parts = [slice(0, half), slice(half, rows)]
    masks = [tri & (seg_col[part] == seg_row[:, part]) for part in parts]
    diagonal = [products[part, part] for part in parts]
    below = jnp.where(seg_col[parts[1]] == seg_row[:, parts[0]], products[parts[1], parts[0]], 0.0).astype(BF16)
    middle = run[half - 1 : half, :]
    entry = jnp.exp(run[parts[1]] - middle)
    leave = jnp.exp(middle - run[parts[0]]) * step_ref[parts[0], :]
    factor = jnp.exp(run)
    skip = skip_ref[model : model + 1, :]
    for p in range(channels // LANES):
        cols = slice(p * LANES, (p + 1) * LANES)
        first = p * lane_head[1]
        x = x_ref[0, :, cols]
        xf = x.astype(F32)
        ys = []
        for part, mask, prod in zip(parts, masks, diagonal):
            y = None
            for k in range(lane_head[1]):
                h = first + k
                mixing = jnp.exp(jnp.where(mask, run[part, h : h + 1] - q[h : h + 1, part], NEG))
                term = dot((mixing * prod).astype(BF16), x[part])
                y = term if y is None else jnp.where(lane_head[0] == k, term, y)
            ys.append(y)
        sent = (xf[parts[0]] * spread(leave, lane_head, first)).astype(BF16)
        ys[1] = ys[1] + dot(below, sent) * spread(entry, lane_head, first)
        y = jnp.concatenate(ys, axis=0) + spread(skip, lane_head, first) * xf
        v = gate_ref[0, :, cols].astype(F32)
        silu = v / (1.0 + jnp.exp(-v))
        yg_ref[:, cols] = y * silu
        fg_ref[:, cols] = (spread(factor, lane_head, first) * silu).astype(BF16)


def inside(model, head_size, x, gate, b, c, run, q, step, skip, seg_row):
    _, rows, channels = x.shape
    heads, state = run.shape[1], b.shape[2]
    at = lambda i: (model, 0, 0)
    whole = lambda i: (0, 0)
    return pl.pallas_call(
        functools.partial(inside_kernel, model, head_size),
        name=f"inside_{model}",
        grid=(1,),
        in_specs=[
            pl.BlockSpec((1, rows, channels), at),
            pl.BlockSpec((1, rows, channels), at),
            pl.BlockSpec((1, rows, state), at),
            pl.BlockSpec((1, rows, state), at),
            pl.BlockSpec((rows, heads), whole),
            pl.BlockSpec((heads, rows), whole),
            pl.BlockSpec((rows, heads), whole),
            pl.BlockSpec(skip.shape, whole),
            pl.BlockSpec(seg_row.shape, whole),
        ],
        out_specs=[pl.BlockSpec((rows, channels), whole), pl.BlockSpec((rows, channels), whole)],
        out_shape=[jax.ShapeDtypeStruct((rows, channels), F32), jax.ShapeDtypeStruct((rows, channels), BF16)],
        compiler_params=PARAMS,
        cost_estimate=cost(2 * rows * rows * LANES * heads, 12 * rows * channels, rows * rows * heads // 2),
    )(x, gate, b, c, run, q, step, skip, seg_row)


def join_kernel(state, own_ref, got_ref, out_ref):
    own, got = own_ref[...].astype(F32), got_ref[...].astype(F32)
    same = (own[state + 2 : state + 3] == got[state + 2 : state + 3]).astype(F32)
    decay = (own[state : state + 1] + own[state + 1 : state + 2]) * same
    out_ref[:state, :] = (own[:state] + decay * got[:state]).astype(BF16)
    out_ref[state:, :] = own_ref[state:, :]


def join(model, state, own, got):
    return pl.pallas_call(
        functools.partial(join_kernel, state),
        name=f"join_{model}",
        out_shape=jax.ShapeDtypeStruct(own.shape, BF16),
        compiler_params=PARAMS,
        cost_estimate=cost(4 * own.size, 6 * own.size),
    )(own, got)


def gate_kernel(model, state, pair_ref, near_ref, *refs):
    far_refs = refs[:-8]
    c_ref, seg_ref, yg_ref, fg_ref, gain_ref, before_ref, g_ref, ss_ref = refs[-8:]
    rows, channels = yg_ref.shape
    paired = pair_ref[0] == 1
    near = near_ref[...].astype(F32)
    far = far_refs[0][...].astype(F32)
    for ref in far_refs[1:]:
        far = far + ref[...].astype(F32)
    last_near, last_far = near[state + 2 : state + 3], far[state + 2 : state + 3]
    decay = (near[state : state + 1] + near[state + 1 : state + 2]) * (last_near == last_far).astype(F32)
    entering = (near[:state] + jnp.where(paired, decay, 1.0) * far[:state]).astype(BF16)
    anchor = jnp.where(paired, last_near, last_far)[:, :1]
    reached = (column(seg_ref[...].astype(F32)) == anchor).astype(F32)
    squares = jnp.zeros((8, rows), F32)
    ones = jnp.ones((8, 512), BF16)
    for p in range(channels // 512):
        cols = slice(p * 512, (p + 1) * 512)
        gated = yg_ref[:, cols] + reached * fg_ref[:, cols].astype(F32) * dot(c_ref[0], entering[:, cols])
        g_ref[:, cols] = (gated * gain_ref[model : model + 1, cols]).astype(BF16)
        squares += lax.dot_general(ones, (gated * gated).astype(BF16), (((1,), (1,)), ((), ())), preferred_element_type=F32)
    ss_ref[...] = jnp.where(lax.broadcasted_iota(jnp.int32, (8, rows), 0) // 4 == model, squares, before_ref[...])


def gate_all(model, pair, near, far, c, seg_row, yg, fg, gain, before):
    rows, channels = yg.shape
    state = c.shape[2]
    whole = lambda i, *_: (0, 0)
    full = lambda a: pl.BlockSpec(a.shape, whole)
    return pl.pallas_call(
        functools.partial(gate_kernel, model, state),
        name=f"gated_{model}",
        grid_spec=pltpu.PrefetchScalarGridSpec(
            num_scalar_prefetch=1,
            grid=(1,),
            in_specs=[full(near)]
            + [full(a) for a in far]
            + [pl.BlockSpec((1, rows, state), lambda i, *_: (model, 0, 0))]
            + [full(a) for a in (seg_row, yg, fg, gain, before)],
            out_specs=[full(yg), pl.BlockSpec((8, rows), whole)],
        ),
        out_shape=[jax.ShapeDtypeStruct((rows, channels), BF16), jax.ShapeDtypeStruct((8, rows), F32)],
        compiler_params=PARAMS,
        cost_estimate=cost(2 * rows * channels * state, 10 * rows * channels),
    )(pair, near, *far, c, seg_row, yg, fg, gain, before)


def project_kernel(kinds, core_ref, *refs):
    count = sum(kinds)
    lhs_refs, (w_ref, keep_ref, send_ref, lhs) = refs[:count], refs[count:]
    half = keep_ref.shape[1]
    chunks = len(kinds)

    @pl.when(pl.program_id(0) == 0)
    def _():
        at = 0
        for i, kind in enumerate(kinds):
            for place, own in ((i, 0), (chunks + i, 1)):
                which = core_ref[0] if own == 0 else 1 - core_ref[0]
                if kind == 1:
                    value = lhs_refs[at][pl.ds(pl.multiple_of(which * half, half), half), :]
                else:
                    value = jnp.where(which == 0, lhs_refs[at][...], lhs_refs[at + 1][...])
                lhs[place * half : (place + 1) * half, :] = value
            at += kind

    result = dot(lhs[...], w_ref[0])
    for i in range(chunks):
        keep_ref[i] = result[i * half : (i + 1) * half]
        send_ref[i] = result[(chunks + i) * half : (chunks + i + 1) * half].astype(BF16)


def project(name, core, model, chunks, w):
    kinds = [len(c) for c in chunks]
    flat = [a for c in chunks for a in c]
    depth, width = w.shape[1:]
    rows = sum(a.shape[0] for a in flat)
    half = rows // len(chunks) // 2
    tile = min(512, width)
    n = len(chunks)
    return pl.pallas_call(
        functools.partial(project_kernel, kinds),
        name=f"{name}_{model}",
        grid_spec=pltpu.PrefetchScalarGridSpec(
            num_scalar_prefetch=1,
            grid=(width // tile,),
            in_specs=[pl.BlockSpec(a.shape, lambda j, *_: (0, 0)) for a in flat]
            + [pl.BlockSpec((1, depth, tile), lambda j, *_: (model, 0, j))],
            out_specs=[pl.BlockSpec((n, half, tile), lambda j, *_: (0, 0, j))] * 2,
            scratch_shapes=[pltpu.VMEM((rows, depth), BF16)],
        ),
        out_shape=[jax.ShapeDtypeStruct((n, half, width), F32), jax.ShapeDtypeStruct((n, half, width), BF16)],
        compiler_params=PARAMS,
        cost_estimate=cost(2 * rows * depth * width, 2 * depth * width + 2 * rows * depth + 6 * n * half * width),
    )(core, *flat, w)


def pair_kernel(order_ref, keep0, got0, keep1, got1, first_ref, second_ref):
    a = keep0[0] + got0[0].astype(F32)
    b = keep1[0] + got1[0].astype(F32)
    turned = order_ref[0] == 1
    first_ref[...] = jnp.where(turned, b, a).astype(BF16)
    second_ref[...] = jnp.where(turned, a, b).astype(BF16)


def pair_sums(name, order, keeps, gots):
    def views(arrays):
        if len(arrays) == 1:
            return [(arrays[0], 0), (arrays[0], 1)]
        return [(arrays[0], 0), (arrays[1], 0)]
    (k0, k1), (g0, g1) = views(keeps), views(gots)
    operands = [k0, g0, k1, g1]
    half, width = keeps[0].shape[1:]
    tile = min(1024, width)
    return pl.pallas_call(
        pair_kernel,
        name=name,
        grid_spec=pltpu.PrefetchScalarGridSpec(
            num_scalar_prefetch=1,
            grid=(width // tile,),
            in_specs=[pl.BlockSpec((1, half, tile), lambda j, *_, i=i: (i, 0, j)) for _, i in operands],
            out_specs=[pl.BlockSpec((half, tile), lambda j, *_: (0, j))] * 2,
        ),
        out_shape=[jax.ShapeDtypeStruct((half, width), BF16)] * 2,
        compiler_params=PARAMS,
        cost_estimate=cost(2 * half * width, 16 * half * width),
    )(order, *[a for a, _ in operands])


def last_kernel(total, model, where_ref, ss_ref, *refs):
    out_ref = refs[-1]
    pieces = refs[-9:-1] if len(refs) >= 9 else refs[:-1]
    half = out_ref.shape[1]
    rows = ss_ref.shape[1]
    core = where_ref[1]
    row = ss_ref[4 * model : 4 * model + 1, :]
    row = jnp.where(core == 0, row[:, :half], row[:, half:])
    scale = column(lax.rsqrt(row / total + EPS))
    own = jnp.where(where_ref[0] == 1, pieces[6][...], pieces[7][...]).astype(F32)
    value = own
    for ref in pieces[:6]:
        value = value + ref[...].astype(F32)
    out_ref[0] = (value * scale).astype(BF16)


def last(model, total, where, ss, pieces, before):
    half, width = pieces[0].shape
    tile = min(1024, width)
    specs = [pl.BlockSpec(ss.shape, lambda j, *_: (0, 0))]
    operands = [ss]
    aliases = {}
    if before is not None:
        specs.append(pl.BlockSpec(memory_space=pl.ANY))
        operands.append(before)
        aliases = {2: 0}
    specs += [pl.BlockSpec((half, tile), lambda j, *_: (0, j))] * len(pieces)
    return pl.pallas_call(
        functools.partial(last_kernel, total, model),
        name=f"last_{model}",
        grid_spec=pltpu.PrefetchScalarGridSpec(
            num_scalar_prefetch=1,
            grid=(width // tile,),
            in_specs=specs,
            out_specs=pl.BlockSpec((1, half, tile), lambda j, *_: (model, 0, j)),
        ),
        out_shape=jax.ShapeDtypeStruct((2, half, width), BF16),
        input_output_aliases=aliases,
        compiler_params=PARAMS,
        cost_estimate=cost(10 * half * width, 18 * half * width),
    )(where, *operands, *pieces)


def xor_pairs(n, k):
    return [(i, i ^ k) for i in range(n)]


def fast(x, gate, b, c, raw, bias, rate, skip, gain, w, seg):
    head_size = x.shape[2] // raw.shape[2]
    state = b.shape[2]
    n_seq, n_head = lax.axis_size("seq"), lax.axis_size("head")
    total = x.shape[2] * n_head
    seg_row = seg.reshape(1, -1)
    s, h = lax.axis_index("seq"), lax.axis_index("head")
    z, core = h // 2, h % 2
    away = jnp.bitwise_xor(s, z)
    one = lambda v: jnp.reshape(v.astype(jnp.int32), (1,))
    core_arr, pair_arr = one(core), one(s % 2)
    order_xy, order_od = one(away % 2), one(1 - away % 2)
    is_od = ((away == 0) | (away == 3)).astype(jnp.int32)
    where = jnp.stack([is_od, core]).astype(jnp.int32)

    def flat(si, zi, ci):
        return si * n_head + zi * 2 + ci

    def sends(kinds, j):
        return [
            (flat(si, si ^ k ^ j, ci), flat(si, si ^ k, ci))
            for si in range(n_seq) for k in kinds for ci in range(2)
        ]

    preps = [prep(m, head_size, x, b, raw, bias, rate, seg_row) for m in range(2)]
    near = [lax.ppermute(preps[m][0], "seq", [(0, 1), (2, 3)]) for m in range(2)]
    insides = [
        inside(m, head_size, x, gate, b, c, preps[m][1], preps[m][2], preps[m][3], skip, seg_row) for m in range(2)
    ]
    joined = [join(m, state, preps[m][0], near[m]) for m in range(2)]
    far = [[lax.ppermute(joined[m], "seq", [(1, t)]) for t in (2, 3)] for m in range(2)]
    ss = jnp.zeros((8, x.shape[1]), F32)
    gs = []
    for m in range(2):
        g, ss = gate_all(m, pair_arr, near[m], far[m], c, seg_row, *insides[m], gain, ss)
        gs.append(g)
    for k in (1, 2, 4):
        ss = ss + lax.ppermute(ss, "head", xor_pairs(n_head, k))
    ss = lax.ppermute(
        ss, ("seq", "head"),
        [(flat(zi, si, ci), flat(si, zi, ci)) for si in range(n_seq) for zi in range(n_seq) for ci in range(2)],
    )
    half = x.shape[1] // 2
    out = None
    for m in range(2):
        g = gs[m]
        px = lax.ppermute(g, "seq", xor_pairs(n_seq, 1))
        py = lax.ppermute(g, "seq", xor_pairs(n_seq, 2))
        d0 = lax.ppermute(px[:half], "seq", xor_pairs(n_seq, 2))
        d1 = lax.ppermute(py[half:], "seq", xor_pairs(n_seq, 1))
        across = lambda a: lax.ppermute(a, "head", xor_pairs(n_head, 1))
        keep_o, send_o = project("own", core_arr, m, [(g,)], w)
        got_o = across(send_o)
        keep_n, send_n = project("next", core_arr, m, [(px,), (py,)], w)
        got_n = across(send_n)
        keep_d, send_d = project("opposite", core_arr, m, [(d0, d1)], w)
        got_d = across(send_d)
        first_n, second_n = pair_sums(f"sum_next_{m}", order_xy, [keep_n], [got_n])
        rest = [
            lax.ppermute(a, ("seq", "head"), sends((1, 2), j)) for a, j in ((first_n, 1), (second_n, 2), (first_n, 3))
        ]
        first_d, second_d = pair_sums(f"sum_opposite_{m}", order_od, [keep_o, keep_d], [got_o, got_d])
        rest += [
            lax.ppermute(a, ("seq", "head"), sends((0, 3), j)) for a, j in ((first_d, 1), (second_d, 2), (first_d, 3))
        ]
        out = last(m, total, where, ss, rest + [second_d, second_n], out)
    return out


def plain(x, gate, b, c, raw, bias, rate, skip, gain, w, seg):
    head_size = x.shape[2] // raw.shape[2]
    state = b.shape[2]
    n_seq, n_head = lax.axis_size("seq"), lax.axis_size("head")
    total = x.shape[2] * n_head
    seg_row = seg.reshape(1, -1)
    s, h = lax.axis_index("seq"), lax.axis_index("head")
    ss = jnp.zeros((8, x.shape[1]), F32)
    gs = []
    for m in range(2):
        msg, run, q, step = prep(m, head_size, x, b, raw, bias, rate, seg_row)
        every = lax.all_gather(msg, "seq").astype(F32)
        entering, before = jnp.zeros_like(every[0]), every[0]
        for k in range(n_seq - 1):
            now = every[k]
            same = (now[state + 2] == before[state + 2]).astype(F32)
            decay = (now[state] + now[state + 1]) * same
            new = jnp.concatenate([now[:state] + decay * entering[:state], now[state:]])
            entering = jnp.where(k < s, new, entering)
            before = now
        yg, fg = inside(m, head_size, x, gate, b, c, run, q, step, skip, seg_row)
        near = entering.astype(BF16)
        g, ss = gate_all(m, jnp.ones((1,), jnp.int32), near, [jnp.zeros_like(near)], c, seg_row, yg, fg, gain, ss)
        gs.append(g)
    g = lax.all_gather(jnp.stack(gs), "seq", axis=1, tiled=True)
    terms = jnp.einsum("mtk,mkd->mtd", g, w, preferred_element_type=F32)
    summed = lax.psum_scatter(terms.astype(BF16), "head", scatter_dimension=1, tiled=True)
    squares = lax.all_gather(lax.psum(ss[::4], "head"), "seq", axis=1, tiled=True)
    mine = lax.dynamic_slice_in_dim(squares, h * summed.shape[1], summed.shape[1], axis=1)
    return (summed.astype(F32) * lax.rsqrt(mine / total + EPS)[:, :, None]).astype(BF16)


def solution(mesh):
    placed = (
        P(None, "seq", "head"),
        P(None, "seq", "head"),
        P(None, "seq", None),
        P(None, "seq", None),
        P(None, "seq", "head"),
        P(None, "head"),
        P(None, "head"),
        P(None, "head"),
        P(None, "head"),
        P(None, "head", "seq"),
        P("seq"),
    )
    local = fast if mesh.shape["seq"] == 4 and mesh.shape["head"] == 8 else plain
    return jax.shard_map(
        local, mesh=mesh, in_specs=placed, out_specs=P(None, "head", "seq"), check_vma=False
    )
```

time: 339 us -> 275 us (0.81)
  waiting for transfers between devices: 215 us -> 71.3 us
  starting transfers between devices: 5.68 us -> 74.4 us
  Pallas kernels: 0 us -> 67.1 us
  local copies, waits for them, and re-layouts: 12 us -> 59.4 us
  matrix products: 47.1 us -> 0 us
  blocking collectives: 24.1 us -> 0 us
  other arithmetic: 21 us -> 0.09 us
  between operations: 13.3 us -> 0.62 us
    all_gather x2 -> x0, waiting for transfers between devices: 125 us -> none  [the longest x1 84.7 us: local(): lax.all_gather(normed, 'seq', axis=1, tiled=True)]
    reduce_scatter x1 -> x0, waiting for transfers between devices: 89.8 us -> none  [local(): lax.psum_scatter(partial_terms.astype(jnp.bfloat16), 'head', scatter_dime...]
    ppermute x1 -> x36, waiting for transfers between devices: 0.01 us -> 71.3 us  [the longest x6 36 us: fast(): lax.ppermute(a, ('seq', 'head'), sends((0, 3), j))]
    ppermute x1 -> x36, starting transfers between devices: 5.33 us -> 74.4 us  [the longest x6 33.5 us: fast(): lax.ppermute(a, ('seq', 'head'), sends((1, 2), j))]
    pallas_call x0 -> x20, Pallas kernels: none -> 67.1 us  [the longest x6 34.1 us: project(): pl.pallas_call(functools.partial(project_kernel, kinds), name=f'{name}_{m...]
    unnamed x26 -> x115, local copies, waits for them, and re-layouts: 3.94 us -> 56.3 us
    dot_general x6 -> x0, matrix products: 47.1 us -> none  [the longest x1 23.9 us: local(): jnp.einsum('mtk,mkd->mtd', lax.all_gather(normed, 'seq', axis=1, tiled=Tr...]
    psum x1 -> x0, blocking collectives: 16.3 us -> none  [local(): square_sum = lax.psum(jnp.sum(gated * gated, axis=2), 'head')]
  transfers between devices with their start and end apart: 4 -> 36, of which waited for: 3 -> 11; matrix products, arithmetic and copies ran while one was open for 3% -> 1% of each run, Pallas kernels for 0% -> 23%
where the time goes in v1:
time: 275 us; the launch traced here: 273 us
  starting transfers between devices  74.4 us (27%)
  waiting for transfers between devices  71.3 us (26%)
  Pallas kernels  67.1 us (24%)
  local copies, waits for them, and re-layouts  59.4 us (22%)
    unnamed x115, local copies, waits for them, and re-layouts  56.3 us
    ppermute x6, waiting for transfers between devices, fast(): lax.ppermute(a, ('seq', 'head'), sends((0, 3), j))  36 us
    pallas_call x6, Pallas kernels, project(): pl.pallas_call(functools.partial(project_kernel, kinds), name=f'{name}_{m...  34.1 us
    ppermute x6, starting transfers between devices, fast(): lax.ppermute(a, ('seq', 'head'), sends((1, 2), j))  33.5 us
    ppermute x2, waiting for transfers between devices, fast(): lax.ppermute(preps[m][0], 'seq', [(0, 1), (2, 3)])  17.5 us
    ppermute x6, starting transfers between devices, fast(): lax.ppermute(a, ('seq', 'head'), sends((0, 3), j))  13.9 us
    pallas_call x2, Pallas kernels, inside(): pl.pallas_call(functools.partial(inside_kernel, model, head_size), name=f...  8.04 us
    ppermute x6, waiting for transfers between devices, fast(): lax.ppermute(a, ('seq', 'head'), sends((1, 2), j))  7.69 us
  transfers between devices with their start and end apart: 36, of which 11 were waited for; matrix products, arithmetic and copies ran while one was open for 1% of the time, Pallas kernels for 23%

profile of v1, /device:TPU:0, one launch (start us, length us, event | category | flops | bytes accessed | tf_op | source)
XLA Modules:
  0.0 272.9 jit_solution(13088586689306730412)
XLA Ops:
  1.0 1.6 copy-done.5
  5.5 2.1 prep_0.1
  8.2 4.9 %collective-permute-start.3 = (bf16[144,2048]{1,0:T(8,128)(2,1)S(1)}, bf16[144,2048]{1,0:T(8,128)(2,1)S(1)}, u32[]{:S(2)}, u32[]{:S(2)}) collective-permute-start(bf16[144,2048]{1,0:T(8,128)(2,1)S(1)} %get-tuple-element.47.own_ref), channel_id=1, source_target_pairs={{0,8},{16,24},{1,9},{17,25},{2,10},{18,26},{3,11},{19,27},{4,12},{... | collective-permute-start | bytes 1769480 | tf_op jit(solution)/shard_map/ppermute | solution.py:400
  13.1 2.1 prep_1.1
  15.3 1.5 collective-permute-start
  16.8 10.0 %collective-permute-done.3.got_ref.near_ref = bf16[144,2048]{1,0:T(8,128)(2,1)S(1)} collective-permute-done((bf16[144,2048]{1,0:T(8,128)(2,1)S(1)}, bf16[144,2048]{1,0:T(8,128)(2,1)S(1)}, u32[]{:S(2)}, u32[]{:S(2)}) %collective-permute-start.3) | collective-permute-done | bytes 589856 | tf_op jit(solution)/shard_map/ppermute | solution.py:400
  27.8 1.5 collective-permute-start.4
  29.3 1.5 collective-permute-start.5
  30.8 7.5 %collective-permute-done.got_ref.near_ref = bf16[144,2048]{1,0:T(8,128)(2,1)S(1)} collective-permute-done((bf16[144,2048]{1,0:T(8,128)(2,1)S(1)}, bf16[144,2048]{1,0:T(8,128)(2,1)S(1)}, u32[]{:S(2)}, u32[]{:S(2)}) %collective-permute-start) | collective-permute-done | bytes 589856 | tf_op jit(solution)/shard_map/ppermute | solution.py:400
  38.3 1.0 join_1.1
  39.3 1.5 collective-permute-start.1
  40.8 1.5 collective-permute-start.2
  42.3 1.6 copy-done.9
  46.5 4.0 %inside_0.1 = (f32[256,2048]{1,0:T(8,128)S(1)}, bf16[256,2048]{1,0:T(8,128)(2,1)S(1)}) custom-call(bf16[2,256,2048]{2,1,0:T(8,128)(2,1)S(1)} %copy-done.6, bf16[2,256,2048]{2,1,0:T(8,128)(2,1)S(1)} %copy-done.9, bf16[2,256,128]{2,1,0:T(8,128)(2,1)S(1)} %copy-done.15, bf16[2,256,128]{2,1,0:T(8,128)(2,1)S(1)} %copy-done.13, f32[256,32]{1,0:T(8,128)S(1)} %copy-done.43, ...), custom_call_target="tpu_custom_call" | custom-call | flops 536870912 | bytes 6291456 | tf_op jit(solution)/shard_map/inside_0/pallas_call | solution.py:159
  50.5 3.2 %gated_0.1 = (bf16[256,2048]{1,0:T(8,128)(2,1)}, f32[8,256]{1,0:T(8,128)S(1)}) custom-call(s32[1]{0:T(128)} %bitcast.2.pair_ref, bf16[144,2048]{1,0:T(8,128)(2,1)S(1)} %collective-permute-done.3.got_ref.near_ref, bf16[144,2048]{1,0:T(8,128)(2,1)} %collective-permute-done.4.refs_0_, bf16[144,2048]{1,0:T(8,128)(2,1)} %collective-permute-done.5.refs_1_, ...), custom_call_target="tpu_custom_call" | custom-call | flops 134217728 | bytes 5242880 | tf_op jit(solution)/shard_map/gated_0/pallas_call | solution.py:228
  53.8 5.2 %collective-permute-start.10 = (bf16[256,2048]{1,0:T(8,128)(2,1)}, bf16[256,2048]{1,0:T(8,128)(2,1)}, u32[]{:S(2)}, u32[]{:S(2)}) collective-permute-start(bf16[256,2048]{1,0:T(8,128)(2,1)} %get-tuple-element.55.refs_0_), channel_id=1, source_target_pairs={{0,8},{8,0},{16,24},{24,16},{1,9},{9,1},{17,25},{25,17},{2,10},{10... | collective-permute-start | bytes 3145736 | tf_op jit(solution)/shard_map/ppermute | solution.py:421
  59.1 4.1 %inside_1.1 = (f32[256,2048]{1,0:T(8,128)S(1)}, bf16[256,2048]{1,0:T(8,128)(2,1)S(1)}) custom-call(bf16[2,256,2048]{2,1,0:T(8,128)(2,1)S(1)} %copy-done.6, bf16[2,256,2048]{2,1,0:T(8,128)(2,1)S(1)} %copy-done.10, bf16[2,256,128]{2,1,0:T(8,128)(2,1)S(1)} %copy-done.15, bf16[2,256,128]{2,1,0:T(8,128)(2,1)S(1)} %copy-done.13, f32[256,32]{1,0:T(8,128)S(1)} %copy-done.39, ...), custom_call_target="tpu_custom_call" | custom-call | flops 536870912 | bytes 6291456 | tf_op jit(solution)/shard_map/inside_1/pallas_call | solution.py:159
  63.2 2.3 gated_1.1
  65.5 2.1 collective-permute-start.24
  67.6 1.2 collective-permute-done.6
  68.7 1.6 collective-permute-start.7
  70.3 5.8 %copy-done = bf16[2,2048,2048]{2,1,0:T(8,128)(2,1)S(1)} copy-done((bf16[2,2048,2048]{2,1,0:T(8,128)(2,1)S(1)}, bf16[2,2048,2048]{2,1,0:T(8,128)(2,1)}, u32[]{:S(2)}) %copy-start) | copy-done | bytes 16777240
  76.1 5.4 %own_0.1 = (f32[1,128,2048]{2,1,0:T(8,128)S(1)}, bf16[1,128,2048]{2,1,0:T(8,128)(2,1)}) custom-call(s32[1]{0:T(128)} %bitcast.1.core_ref, bf16[256,2048]{1,0:T(8,128)(2,1)} %get-tuple-element.55.refs_0_, bf16[2,2048,2048]{2,1,0:T(8,128)(2,1)S(1)} %copy-done), custom_call_target="tpu_custom_call" | custom-call | flops 2147483648 | bytes 11010048 | tf_op jit(solution)/shard_map/own_0/pallas_call | solution.py:279
  81.5 2.0 collective-permute-done.10.refs_0_
  83.4 1.1 slice.16
  85.4 1.1 slice.17
  86.5 1.2 collective-permute-start.18
  87.8 5.8 %copy-done.1 = bf16[2,2048,2048]{2,1,0:T(8,128)(2,1)S(1)} copy-done((bf16[2,2048,2048]{2,1,0:T(8,128)(2,1)S(1)}, bf16[2,2048,2048]{2,1,0:T(8,128)(2,1)}, u32[]{:S(2)}) %copy-start.1) | copy-done | bytes 16777240
  93.6 8.0 %next_0.1 = (f32[2,128,2048]{2,1,0:T(8,128)S(1)}, bf16[2,128,2048]{2,1,0:T(8,128)(2,1)}) custom-call(s32[1]{0:T(128)} %bitcast.1.core_ref, bf16[256,2048]{1,0:T(8,128)(2,1)} %collective-permute-done.10.refs_0_, bf16[256,2048]{1,0:T(8,128)(2,1)} %collective-permute-done.11.refs_1_, bf16[2,2048,2048]{2,1,0:T(8,128)(2,1)S(1)} %copy-done.1), custom_call_target="tpu_custom_call" | custom-call | flops 4294967296 | bytes 13631488 | tf_op jit(solution)/shard_map/next_0/pallas_call | solution.py:279
  101.6 4.2 %collective-permute-done.23.refs_0_ = bf16[256,2048]{1,0:T(8,128)(2,1)S(1)} collective-permute-done((bf16[256,2048]{1,0:T(8,128)(2,1)S(1)}, bf16[256,2048]{1,0:T(8,128)(2,1)S(1)}, u32[]{:S(2)}, u32[]{:S(2)}) %collective-permute-start.23) | collective-permute-done | bytes 1048608 | tf_op jit(solution)/shard_map/ppermute | solution.py:421
  105.9 1.9 collective-permute-done.24.refs_1_
  109.8 5.8 %copy-done.2 = bf16[2,2048,2048]{2,1,0:T(8,128)(2,1)S(1)} copy-done((bf16[2,2048,2048]{2,1,0:T(8,128)(2,1)S(1)}, bf16[2,2048,2048]{2,1,0:T(8,128)(2,1)}, u32[]{:S(2)}) %copy-start.2) | copy-done | bytes 16777240
  115.6 1.2 copy-done.12
  116.8 6.7 %next_1.1 = (f32[2,128,2048]{2,1,0:T(8,128)S(1)}, bf16[2,128,2048]{2,1,0:T(8,128)(2,1)}) custom-call(s32[1]{0:T(128)} %bitcast.1.core_ref, bf16[256,2048]{1,0:T(8,128)(2,1)S(1)} %collective-permute-done.23.refs_0_, bf16[256,2048]{1,0:T(8,128)(2,1)S(1)} %copy-done.12, bf16[2,2048,2048]{2,1,0:T(8,128)(2,1)S(1)} %copy-done.2), custom_call_target="tpu_custom_call" | custom-call | flops 4294967296 | bytes 13631488 | tf_op jit(solution)/shard_map/next_1/pallas_call | solution.py:279
  123.5 2.6 collective-permute-start.8
  126.1 4.3 %opposite_0.1 = (f32[1,128,2048]{2,1,0:T(8,128)S(1)}, bf16[1,128,2048]{2,1,0:T(8,128)(2,1)}) custom-call(s32[1]{0:T(128)} %bitcast.1.core_ref, bf16[128,2048]{1,0:T(8,128)(2,1)S(1)} %collective-permute-done.17.refs_0_, bf16[128,2048]{1,0:T(8,128)(2,1)S(1)} %collective-permute-done.18.refs_1_, bf16[2,2048,2048]{2,1,0:T(8,128)(2,1)S(1)} %copy-done.2), custom_call_target="tpu_custom_call" | custom-call | flops 2147483648 | bytes 11010048 | tf_op jit(solution)/shard_map/opposite_0/pallas_call | solution.py:279
  130.4 1.1 copy-done.20
  132.8 5.8 %copy-done.3 = bf16[2,2048,2048]{2,1,0:T(8,128)(2,1)S(1)} copy-done((bf16[2,2048,2048]{2,1,0:T(8,128)(2,1)S(1)}, bf16[2,2048,2048]{2,1,0:T(8,128)(2,1)}, u32[]{:S(2)}) %copy-start.3) | copy-done | bytes 16777240
  138.5 1.2 copy-done.17
  139.8 4.3 %own_1.1 = (f32[1,128,2048]{2,1,0:T(8,128)S(1)}, bf16[1,128,2048]{2,1,0:T(8,128)(2,1)}) custom-call(s32[1]{0:T(128)} %bitcast.1.core_ref, bf16[256,2048]{1,0:T(8,128)(2,1)S(1)} %copy-done.17, bf16[2,2048,2048]{2,1,0:T(8,128)(2,1)S(1)} %copy-done.3), custom_call_target="tpu_custom_call" | custom-call | flops 2147483648 | bytes 11010048 | tf_op jit(solution)/shard_map/own_1/pallas_call | solution.py:279
  145.8 5.8 %copy-done.4 = bf16[2,2048,2048]{2,1,0:T(8,128)(2,1)S(1)} copy-done((bf16[2,2048,2048]{2,1,0:T(8,128)(2,1)S(1)}, bf16[2,2048,2048]{2,1,0:T(8,128)(2,1)}, u32[]{:S(2)}) %copy-start.4) | copy-done | bytes 16777240
  151.5 5.3 %opposite_1.1 = (f32[1,128,2048]{2,1,0:T(8,128)S(1)}, bf16[1,128,2048]{2,1,0:T(8,128)(2,1)}) custom-call(s32[1]{0:T(128)} %bitcast.1.core_ref, bf16[128,2048]{1,0:T(8,128)(2,1)S(1)} %copy-done.27, bf16[128,2048]{1,0:T(8,128)(2,1)} %collective-permute-done.31.refs_1_, bf16[2,2048,2048]{2,1,0:T(8,128)(2,1)S(1)} %copy-done.4), custom_call_target="tpu_custom_call" | custom-call | flops 2147483648 | bytes 11010048 | tf_op jit(solution)/shard_map/opposite_1/pallas_call | solution.py:279
  157.5 2.2 sum_next_0.1
  159.7 7.2 %collective-permute-start.13 = (bf16[128,2048]{1,0:T(8,128)(2,1)}, bf16[128,2048]{1,0:T(8,128)(2,1)}, u32[]{:S(2)}, u32[]{:S(2)}) collective-permute-start(bf16[128,2048]{1,0:T(8,128)(2,1)} %get-tuple-element.58), channel_id=1, source_target_pairs={{0,2},{1,3},{6,4},{7,5},{10,8},{11,9},{12,14},{13,15},{20,22},{21,... | collective-permute-start | bytes 1572872 | tf_op jit(solution)/shard_map/ppermute | solution.py:434
  166.9 2.3 collective-permute-start.14
  169.2 1.2 copy-done.19
  170.4 1.2 copy-done.21
  171.7 1.4 sum_opposite_0.1
  173.8 1.3 collective-permute-start.20
  175.2 1.3 collective-permute-start.21
  176.5 1.4 sum_next_1.1
  178.7 4.4 %collective-permute-start.22 = (bf16[128,2048]{1,0:T(8,128)(2,1)S(1)}, bf16[128,2048]{1,0:T(8,128)(2,1)S(1)}, u32[]{:S(2)}, u32[]{:S(2)}) collective-permute-start(bf16[128,2048]{1,0:T(8,128)(2,1)S(1)} %get-tuple-element.64), channel_id=1, source_target_pairs={{6,0},{7,1},{0,6},{1,7},{12,10},{13,11},{10,12},{11,13},{18,20},{1... | collective-permute-start | bytes 1572872 | tf_op jit(solution)/shard_map/ppermute | solution.py:438
  183.0 6.9 %collective-permute-done.14.refs_1_ = bf16[128,2048]{1,0:T(8,128)(2,1)} collective-permute-done((bf16[128,2048]{1,0:T(8,128)(2,1)}, bf16[128,2048]{1,0:T(8,128)(2,1)}, u32[]{:S(2)}, u32[]{:S(2)}) %collective-permute-start.14) | collective-permute-done | bytes 524320 | tf_op jit(solution)/shard_map/ppermute | solution.py:434
  190.0 5.5 %collective-permute-start.26 = (bf16[128,2048]{1,0:T(8,128)(2,1)}, bf16[128,2048]{1,0:T(8,128)(2,1)S(1)}, u32[]{:S(2)}, u32[]{:S(2)}) collective-permute-start(bf16[128,2048]{1,0:T(8,128)(2,1)} %get-tuple-element.69), channel_id=1, source_target_pairs={{0,2},{1,3},{6,4},{7,5},{10,8},{11,9},{12,14},{13,15},{20,22},{21,... | collective-permute-start | bytes 1572872 | tf_op jit(solution)/shard_map/ppermute | solution.py:434
  195.4 2.1 sum_opposite_1.1
  199.9 17.1 %collective-permute-start.27 = (bf16[128,2048]{1,0:T(8,128)(2,1)}, bf16[128,2048]{1,0:T(8,128)(2,1)S(1)}, u32[]{:S(2)}, u32[]{:S(2)}) collective-permute-start(bf16[128,2048]{1,0:T(8,128)(2,1)} %get-tuple-element.70.refs_8_), channel_id=1, source_target_pairs={{6,2},{7,3},{0,4},{1,5},{12,8},{13,9},{10,14},{11,15},{18,22},{19,... | collective-permute-start | bytes 1572872 | tf_op jit(solution)/shard_map/ppermute | solution.py:434
  217.0 15.0 %collective-permute-done.21.refs_4_ = bf16[128,2048]{1,0:T(8,128)(2,1)S(1)} collective-permute-done((bf16[128,2048]{1,0:T(8,128)(2,1)S(1)}, bf16[128,2048]{1,0:T(8,128)(2,1)S(1)}, u32[]{:S(2)}, u32[]{:S(2)}) %collective-permute-start.21) | collective-permute-done | bytes 524320 | tf_op jit(solution)/shard_map/ppermute | solution.py:438
  232.8 1.3 collective-permute-start.33
  234.9 1.3 collective-permute-start.34
  236.2 4.4 %collective-permute-start.35 = (bf16[128,2048]{1,0:T(8,128)(2,1)}, bf16[128,2048]{1,0:T(8,128)(2,1)}, u32[]{:S(2)}, u32[]{:S(2)}) collective-permute-start(bf16[128,2048]{1,0:T(8,128)(2,1)} %get-tuple-element.75), channel_id=1, source_target_pairs={{6,0},{7,1},{0,6},{1,7},{12,10},{13,11},{10,12},{11,13},{18,20},{1... | collective-permute-start | bytes 1572872 | tf_op jit(solution)/shard_map/ppermute | solution.py:438
  240.6 1.0 copy-done.29
  245.8 3.1 %last_0.1.refs_0_ = bf16[2,128,2048]{2,1,0:T(8,128)(2,1)} custom-call(s32[2]{0:T(128)S(1)} %pad_add_fusion.where_ref, f32[8,256]{1,0:T(8,128)S(1)} %collective-permute-done.9.ss_ref, bf16[128,2048]{1,0:T(8,128)(2,1)} %collective-permute-done.13.refs_0_, bf16[128,2048]{1,0:T(8,128)(2,1)} %collective-permute-done.14.refs_1_, bf16[128,2048]{1,0:T(8,128)(2,1)S(1)} %copy-done.31, ...), custom_call_target="tpu_custom_call" | custom-call | flops 2621440 | bytes 4718592 | tf_op jit(solution)/shard_map/last_0/pallas_call | solution.py:355
  248.9 21.0 %collective-permute-done.33.refs_4_ = bf16[128,2048]{1,0:T(8,128)(2,1)S(1)} collective-permute-done((bf16[128,2048]{1,0:T(8,128)(2,1)}, bf16[128,2048]{1,0:T(8,128)(2,1)S(1)}, u32[]{:S(2)}, u32[]{:S(2)}) %collective-permute-start.33) | collective-permute-done | bytes 524320 | tf_op jit(solution)/shard_map/ppermute | solution.py:438
  269.9 3.1 %last_1.1 = bf16[2,128,2048]{2,1,0:T(8,128)(2,1)} custom-call(s32[2]{0:T(128)S(1)} %pad_add_fusion.where_ref, f32[8,256]{1,0:T(8,128)S(1)} %collective-permute-done.9.ss_ref, bf16[2,128,2048]{2,1,0:T(8,128)(2,1)} %last_0.1.refs_0_, bf16[128,2048]{1,0:T(8,128)(2,1)S(1)} %collective-permute-done.26.refs_1_, ...), custom_call_target="tpu_custom_call", output_to_operand_aliasing={{}: (2, {})} | custom-call | flops 2621440 | bytes 4718592 | tf_op jit(solution)/shard_map/last_1/pallas_call | solution.py:355
  (152 shorter events, 24.5 us)
Async XLA Ops:
  0.0 13.1 %copy-start.55 = (f32[2,32]{1,0:T(2,128)S(1)}, f32[2,32]{1,0:T(2,128)}, u32[]{:S(2)}) copy-start(f32[2,32]{1,0:T(2,128)} %rate_ref.3) | copy-start | bytes 772
  0.0 13.1 %copy-start.48 = (s32[256]{0:T(256)S(1)}, s32[256]{0:T(256)}, u32[]{:S(2)}) copy-start(s32[256]{0:T(256)} %param.21) | copy-start | bytes 3076
  8.2 19.6 %copy-start.42 = (f32[256,32]{1,0:T(8,128)}, f32[256,32]{1,0:T(8,128)S(1)}, u32[]{:S(2)}) copy-start(f32[256,32]{1,0:T(8,128)S(1)} %get-tuple-element.48.run_ref) | copy-start | bytes 98308
  8.2 19.6 %copy-start.44 = (f32[256,32]{1,0:T(8,128)}, f32[256,32]{1,0:T(8,128)S(1)}, u32[]{:S(2)}) copy-start(f32[256,32]{1,0:T(8,128)S(1)} %get-tuple-element.50.step_ref) | copy-start | bytes 98308
  8.2 18.6 %collective-permute-start.3 = (bf16[144,2048]{1,0:T(8,128)(2,1)S(1)}, bf16[144,2048]{1,0:T(8,128)(2,1)S(1)}, u32[]{:S(2)}, u32[]{:S(2)}) collective-permute-start(bf16[144,2048]{1,0:T(8,128)(2,1)S(1)} %get-tuple-element.47.own_ref), channel_id=1, source_target_pairs={{0,8},{16,24},{1,9},{17,25},{2,10},{18,26},{3,11},{19,27},{4,12},{... | collective-permute-start | bytes 1769480 | tf_op jit(solution)/shard_map/ppermute | solution.py:400
  15.2 24.1 %copy-start.38 = (f32[256,32]{1,0:T(8,128)}, f32[256,32]{1,0:T(8,128)S(1)}, u32[]{:S(2)}) copy-start(f32[256,32]{1,0:T(8,128)S(1)} %get-tuple-element.42.run_ref) | copy-start | bytes 98308
  15.2 25.6 %copy-start.40 = (f32[256,32]{1,0:T(8,128)}, f32[256,32]{1,0:T(8,128)S(1)}, u32[]{:S(2)}) copy-start(f32[256,32]{1,0:T(8,128)S(1)} %get-tuple-element.44.step_ref) | copy-start | bytes 98308
  15.3 27.0 %copy-start.49 = (f32[32,256]{1,0:T(8,128)}, f32[32,256]{1,0:T(8,128)S(1)}, u32[]{:S(2)}) copy-start(f32[32,256]{1,0:T(8,128)S(1)} %get-tuple-element.43.q_ref) | copy-start | bytes 98308
  15.3 27.0 %copy-start.6 = (bf16[2,256,2048]{2,1,0:T(8,128)(2,1)S(1)}, bf16[2,256,2048]{2,1,0:T(8,128)(2,1)}, u32[]{:S(2)}) copy-start(bf16[2,256,2048]{2,1,0:T(8,128)(2,1)} %x_ref.7) | copy-start | bytes 6291460
  15.3 27.0 %copy-start.13 = (bf16[2,256,128]{2,1,0:T(8,128)(2,1)S(1)}, bf16[2,256,128]{2,1,0:T(8,128)(2,1)}, u32[]{:S(2)}) copy-start(bf16[2,256,128]{2,1,0:T(8,128)(2,1)} %refs_2_.7) | copy-start | bytes 393220
  15.3 27.0 %copy-start.15 = (bf16[2,256,128]{2,1,0:T(8,128)(2,1)S(1)}, bf16[2,256,128]{2,1,0:T(8,128)(2,1)}, u32[]{:S(2)}) copy-start(bf16[2,256,128]{2,1,0:T(8,128)(2,1)} %b_ref.7) | copy-start | bytes 393220
  15.3 27.0 %copy-start.56 = (f32[2,32]{1,0:T(2,128)S(1)}, f32[2,32]{1,0:T(2,128)}, u32[]{:S(2)}) copy-start(f32[2,32]{1,0:T(2,128)} %skip_ref.3) | copy-start | bytes 772
  15.3 23.0 %collective-permute-start = (bf16[144,2048]{1,0:T(8,128)(2,1)S(1)}, bf16[144,2048]{1,0:T(8,128)(2,1)S(1)}, u32[]{:S(2)}, u32[]{:S(2)}) collective-permute-start(bf16[144,2048]{1,0:T(8,128)(2,1)S(1)} %get-tuple-element.41.own_ref), channel_id=1, source_target_pairs={{0,8},{16,24},{1,9},{17,25},{2,10},{18,26},{3,11},{19,27},{4,12},{... | collective-permute-start | bytes 1769480 | tf_op jit(solution)/shard_map/ppermute | solution.py:400
  27.8 22.6 %collective-permute-start.4 = (bf16[144,2048]{1,0:T(8,128)(2,1)}, bf16[144,2048]{1,0:T(8,128)(2,1)}, u32[]{:S(2)}, u32[]{:S(2)}) collective-permute-start(bf16[144,2048]{1,0:T(8,128)(2,1)} %join_0.1), channel_id=1, source_target_pairs={{8,16},{9,17},{10,18},{11,19},{12,20},{13,21},{14,22},{15,23}} | collective-permute-start | bytes 1769480 | tf_op jit(solution)/shard_map/ppermute | solution.py:405
  29.3 21.1 %collective-permute-start.5 = (bf16[144,2048]{1,0:T(8,128)(2,1)}, bf16[144,2048]{1,0:T(8,128)(2,1)}, u32[]{:S(2)}, u32[]{:S(2)}) collective-permute-start(bf16[144,2048]{1,0:T(8,128)(2,1)} %join_0.1), channel_id=1, source_target_pairs={{8,24},{9,25},{10,26},{11,27},{12,28},{13,29},{14,30},{15,31}} | collective-permute-start | bytes 1769480 | tf_op jit(solution)/shard_map/ppermute | solution.py:405
  39.3 23.8 %collective-permute-start.1 = (bf16[144,2048]{1,0:T(8,128)(2,1)}, bf16[144,2048]{1,0:T(8,128)(2,1)}, u32[]{:S(2)}, u32[]{:S(2)}) collective-permute-start(bf16[144,2048]{1,0:T(8,128)(2,1)} %join_1.1), channel_id=1, source_target_pairs={{8,16},{9,17},{10,18},{11,19},{12,20},{13,21},{14,22},{15,23}} | collective-permute-start | bytes 1769480 | tf_op jit(solution)/shard_map/ppermute | solution.py:405
  40.8 22.3 %collective-permute-start.2 = (bf16[144,2048]{1,0:T(8,128)(2,1)}, bf16[144,2048]{1,0:T(8,128)(2,1)}, u32[]{:S(2)}, u32[]{:S(2)}) collective-permute-start(bf16[144,2048]{1,0:T(8,128)(2,1)} %join_1.1), channel_id=1, source_target_pairs={{8,24},{9,25},{10,26},{11,27},{12,28},{13,29},{14,30},{15,31}} | collective-permute-start | bytes 1769480 | tf_op jit(solution)/shard_map/ppermute | solution.py:405
  50.5 8.5 %copy-start.10 = (bf16[2,256,2048]{2,1,0:T(8,128)(2,1)S(1)}, bf16[2,256,2048]{2,1,0:T(8,128)(2,1)}, u32[]{:S(2)}) copy-start(bf16[2,256,2048]{2,1,0:T(8,128)(2,1)} %gate_ref.3) | copy-start | bytes 6291460
  50.5 8.5 %copy-start.39 = (f32[256,32]{1,0:T(8,128)S(1)}, f32[256,32]{1,0:T(8,128)}, u32[]{:S(2)}) copy-start(f32[256,32]{1,0:T(8,128)} %copy-done.38) | copy-start | bytes 98308
  50.5 8.5 %copy-start.41 = (f32[256,32]{1,0:T(8,128)S(1)}, f32[256,32]{1,0:T(8,128)}, u32[]{:S(2)}) copy-start(f32[256,32]{1,0:T(8,128)} %copy-done.40) | copy-start | bytes 98308
  50.5 8.5 %copy-start.50 = (f32[32,256]{1,0:T(8,128)S(1)}, f32[32,256]{1,0:T(8,128)}, u32[]{:S(2)}) copy-start(f32[32,256]{1,0:T(8,128)} %copy-done.49) | copy-start | bytes 98308
  53.8 29.6 %collective-permute-start.10 = (bf16[256,2048]{1,0:T(8,128)(2,1)}, bf16[256,2048]{1,0:T(8,128)(2,1)}, u32[]{:S(2)}, u32[]{:S(2)}) collective-permute-start(bf16[256,2048]{1,0:T(8,128)(2,1)} %get-tuple-element.55.refs_0_), channel_id=1, source_target_pairs={{0,8},{8,0},{16,24},{24,16},{1,9},{9,1},{17,25},{25,17},{2,10},{10... | collective-permute-start | bytes 3145736 | tf_op jit(solution)/shard_map/ppermute | solution.py:421
  59.0 26.4 %collective-permute-start.11 = (bf16[256,2048]{1,0:T(8,128)(2,1)}, bf16[256,2048]{1,0:T(8,128)(2,1)}, u32[]{:S(2)}, u32[]{:S(2)}) collective-permute-start(bf16[256,2048]{1,0:T(8,128)(2,1)} %get-tuple-element.55.refs_0_), channel_id=1, source_target_pairs={{0,16},{8,24},{16,0},{24,8},{1,17},{9,25},{17,1},{25,9},{2,18},{10... | collective-permute-start | bytes 3145736 | tf_op jit(solution)/shard_map/ppermute | solution.py:422
  65.5 16.0 %copy-start.16 = (bf16[256,2048]{1,0:T(8,128)(2,1)}, bf16[256,2048]{1,0:T(8,128)(2,1)S(1)}, u32[]{:S(2)}) copy-start(bf16[256,2048]{1,0:T(8,128)(2,1)S(1)} %get-tuple-element.66.refs_0_) | copy-start | bytes 3145732
  65.5 40.3 %collective-permute-start.23 = (bf16[256,2048]{1,0:T(8,128)(2,1)S(1)}, bf16[256,2048]{1,0:T(8,128)(2,1)S(1)}, u32[]{:S(2)}, u32[]{:S(2)}) collective-permute-start(bf16[256,2048]{1,0:T(8,128)(2,1)S(1)} %get-tuple-element.66.refs_0_), channel_id=1, source_target_pairs={{0,8},{8,0},{16,24},{24,16},{1,9},{9,1},{17,25},{25,17},{2,10},{10... | collective-permute-start | bytes 3145736 | tf_op jit(solution)/shard_map/ppermute | solution.py:421
  65.5 42.3 %collective-permute-start.24 = (bf16[256,2048]{1,0:T(8,128)(2,1)S(1)}, bf16[256,2048]{1,0:T(8,128)(2,1)S(1)}, u32[]{:S(2)}, u32[]{:S(2)}) collective-permute-start(bf16[256,2048]{1,0:T(8,128)(2,1)S(1)} %get-tuple-element.66.refs_0_), channel_id=1, source_target_pairs={{0,16},{8,24},{16,0},{24,8},{1,17},{9,25},{17,1},{25,9},{2,18},{10... | collective-permute-start | bytes 3145736 | tf_op jit(solution)/shard_map/ppermute | solution.py:422
  67.6 1.2 collective-permute-start.6
  68.7 12.7 %collective-permute-start.7 = (f32[8,256]{1,0:T(8,128)S(1)}, f32[8,256]{1,0:T(8,128)S(1)}, u32[]{:S(2)}, u32[]{:S(2)}) collective-permute-start(f32[8,256]{1,0:T(8,128)S(1)} %add.23), channel_id=1, source_target_pairs={{0,2},{1,3},{2,0},{3,1},{4,6},{5,7},{6,4},{7,5},{8,10},{9,11},{10,... | collective-permute-start | bytes 24584 | tf_op jit(solution)/shard_map/ppermute | solution.py:412
  70.3 5.8 %copy-start = (bf16[2,2048,2048]{2,1,0:T(8,128)(2,1)S(1)}, bf16[2,2048,2048]{2,1,0:T(8,128)(2,1)}, u32[]{:S(2)}) copy-start(bf16[2,2048,2048]{2,1,0:T(8,128)(2,1)} %refs_2_.11) | copy-start | bytes 50331652
  81.4 5.1 %copy-start.18 = (f32[1,128,2048]{2,1,0:T(8,128)}, f32[1,128,2048]{2,1,0:T(8,128)S(1)}, u32[]{:S(2)}) copy-start(f32[1,128,2048]{2,1,0:T(8,128)S(1)} %get-tuple-element.60.keep0) | copy-start | bytes 3145732
  84.5 39.0 %collective-permute-start.17 = (bf16[128,2048]{1,0:T(8,128)(2,1)S(1)}, bf16[128,2048]{1,0:T(8,128)(2,1)S(1)}, u32[]{:S(2)}, u32[]{:S(2)}) collective-permute-start(bf16[128,2048]{1,0:T(8,128)(2,1)S(1)} %slice.16), channel_id=1, source_target_pairs={{0,16},{8,24},{16,0},{24,8},{1,17},{9,25},{17,1},{25,9},{2,18},{10... | collective-permute-start | bytes 1572872 | tf_op jit(solution)/shard_map/ppermute | solution.py:423
  86.5 39.5 %collective-permute-start.18 = (bf16[128,2048]{1,0:T(8,128)(2,1)S(1)}, bf16[128,2048]{1,0:T(8,128)(2,1)S(1)}, u32[]{:S(2)}, u32[]{:S(2)}) collective-permute-start(bf16[128,2048]{1,0:T(8,128)(2,1)S(1)} %slice.17), channel_id=1, source_target_pairs={{0,8},{8,0},{16,24},{24,16},{1,9},{9,1},{17,25},{25,17},{2,10},{10... | collective-permute-start | bytes 1572872 | tf_op jit(solution)/shard_map/ppermute | solution.py:424
  87.8 5.8 %copy-start.1 = (bf16[2,2048,2048]{2,1,0:T(8,128)(2,1)S(1)}, bf16[2,2048,2048]{2,1,0:T(8,128)(2,1)}, u32[]{:S(2)}) copy-start(bf16[2,2048,2048]{2,1,0:T(8,128)(2,1)} %refs_2_.11) | copy-start | bytes 50331652
  101.6 21.9 %copy-start.7 = (f32[2,128,2048]{2,1,0:T(8,128)}, f32[2,128,2048]{2,1,0:T(8,128)S(1)}, u32[]{:S(2)}) copy-start(f32[2,128,2048]{2,1,0:T(8,128)S(1)} %get-tuple-element.56.keep0.keep1) | copy-start | bytes 6291460
  101.6 55.8 %collective-permute-start.12 = (bf16[2,128,2048]{2,1,0:T(8,128)(2,1)}, bf16[2,128,2048]{2,1,0:T(8,128)(2,1)}, u32[]{:S(2)}, u32[]{:S(2)}) collective-permute-start(bf16[2,128,2048]{2,1,0:T(8,128)(2,1)} %get-tuple-element.57), channel_id=1, source_target_pairs={{0,1},{1,0},{2,3},{3,2},{4,5},{5,4},{6,7},{7,6},{8,9},{9,8},{10,11... | collective-permute-start | bytes 3145736 | tf_op jit(solution)/shard_map/ppermute | solution.py:425
  105.8 26.1 %collective-permute-start.30 = (bf16[128,2048]{1,0:T(8,128)(2,1)S(1)}, bf16[128,2048]{1,0:T(8,128)(2,1)S(1)}, u32[]{:S(2)}, u32[]{:S(2)}) collective-permute-start(bf16[128,2048]{1,0:T(8,128)(2,1)S(1)} %slice.18), channel_id=1, source_target_pairs={{0,16},{8,24},{16,0},{24,8},{1,17},{9,25},{17,1},{25,9},{2,18},{10... | collective-permute-start | bytes 1572872 | tf_op jit(solution)/shard_map/ppermute | solution.py:423
  109.7 35.4 %collective-permute-start.31 = (bf16[128,2048]{1,0:T(8,128)(2,1)}, bf16[128,2048]{1,0:T(8,128)(2,1)}, u32[]{:S(2)}, u32[]{:S(2)}) collective-permute-start(bf16[128,2048]{1,0:T(8,128)(2,1)} %slice.19), channel_id=1, source_target_pairs={{0,8},{8,0},{16,24},{24,16},{1,9},{9,1},{17,25},{25,17},{2,10},{10... | collective-permute-start | bytes 1572872 | tf_op jit(solution)/shard_map/ppermute | solution.py:424
  109.8 5.8 %copy-start.2 = (bf16[2,2048,2048]{2,1,0:T(8,128)(2,1)S(1)}, bf16[2,2048,2048]{2,1,0:T(8,128)(2,1)}, u32[]{:S(2)}) copy-start(bf16[2,2048,2048]{2,1,0:T(8,128)(2,1)} %refs_2_.11) | copy-start | bytes 50331652
  123.5 8.0 %collective-permute-start.8 = (f32[8,256]{1,0:T(8,128)S(1)}, f32[8,256]{1,0:T(8,128)S(1)}, u32[]{:S(2)}, u32[]{:S(2)}) collective-permute-start(f32[8,256]{1,0:T(8,128)S(1)} %add.24), channel_id=1, source_target_pairs={{0,4},{1,5},{2,6},{3,7},{4,0},{5,1},{6,2},{7,3},{8,12},{9,13},{10,... | collective-permute-start | bytes 24584 | tf_op jit(solution)/shard_map/ppermute | solution.py:412
  126.1 47.8 %collective-permute-start.25 = (bf16[2,128,2048]{2,1,0:T(8,128)(2,1)}, bf16[2,128,2048]{2,1,0:T(8,128)(2,1)S(1)}, u32[]{:S(2)}, u32[]{:S(2)}) collective-permute-start(bf16[2,128,2048]{2,1,0:T(8,128)(2,1)} %get-tuple-element.68), channel_id=1, source_target_pairs={{0,1},{1,0},{2,3},{3,2},{4,5},{5,4},{6,7},{7,6},{8,9},{9,8},{10,11... | collective-permute-start | bytes 3145736 | tf_op jit(solution)/shard_map/ppermute | solution.py:425
  131.5 28.2 %collective-permute-start.16 = (bf16[1,128,2048]{2,1,0:T(8,128)(2,1)}, bf16[1,128,2048]{2,1,0:T(8,128)(2,1)}, u32[]{:S(2)}, u32[]{:S(2)}) collective-permute-start(bf16[1,128,2048]{2,1,0:T(8,128)(2,1)} %get-tuple-element.61), channel_id=1, source_target_pairs={{0,1},{1,0},{2,3},{3,2},{4,5},{5,4},{6,7},{7,6},{8,9},{9,8},{10,11... | collective-permute-start | bytes 1572872 | tf_op jit(solution)/shard_map/ppermute | solution.py:425
  132.8 34.1 %collective-permute-start.19 = (bf16[1,128,2048]{2,1,0:T(8,128)(2,1)}, bf16[1,128,2048]{2,1,0:T(8,128)(2,1)}, u32[]{:S(2)}, u32[]{:S(2)}) collective-permute-start(bf16[1,128,2048]{2,1,0:T(8,128)(2,1)} %get-tuple-element.63), channel_id=1, source_target_pairs={{0,1},{1,0},{2,3},{3,2},{4,5},{5,4},{6,7},{7,6},{8,9},{9,8},{10,11... | collective-permute-start | bytes 1572872 | tf_op jit(solution)/shard_map/ppermute | solution.py:425
  132.8 5.8 %copy-start.3 = (bf16[2,2048,2048]{2,1,0:T(8,128)(2,1)S(1)}, bf16[2,2048,2048]{2,1,0:T(8,128)(2,1)}, u32[]{:S(2)}) copy-start(bf16[2,2048,2048]{2,1,0:T(8,128)(2,1)} %refs_2_.11) | copy-start | bytes 50331652
  139.8 6.0 %copy-start.27 = (bf16[128,2048]{1,0:T(8,128)(2,1)S(1)}, bf16[128,2048]{1,0:T(8,128)(2,1)}, u32[]{:S(2)}) copy-start(bf16[128,2048]{1,0:T(8,128)(2,1)} %copy-done.26) | copy-start | bytes 1572868
  145.1 11.8 %collective-permute-start.9 = (f32[8,256]{1,0:T(8,128)S(1)}, f32[8,256]{1,0:T(8,128)S(1)}, u32[]{:S(2)}, u32[]{:S(2)}) collective-permute-start(f32[8,256]{1,0:T(8,128)S(1)} %add.25), channel_id=1, source_target_pairs={{0,0},{1,1},{8,2},{9,3},{16,4},{17,5},{24,6},{25,7},{2,8},{3,9},{1... | collective-permute-start | bytes 24584 | tf_op jit(solution)/shard_map/ppermute | solution.py:413
  145.8 5.8 %copy-start.4 = (bf16[2,2048,2048]{2,1,0:T(8,128)(2,1)S(1)}, bf16[2,2048,2048]{2,1,0:T(8,128)(2,1)}, u32[]{:S(2)}) copy-start(bf16[2,2048,2048]{2,1,0:T(8,128)(2,1)} %refs_2_.11) | copy-start | bytes 50331652
  151.5 5.9 %copy-start.8 = (f32[2,128,2048]{2,1,0:T(8,128)S(1)}, f32[2,128,2048]{2,1,0:T(8,128)}, u32[]{:S(2)}) copy-start(f32[2,128,2048]{2,1,0:T(8,128)} %copy-done.7) | copy-start | bytes 6291460
  156.9 16.2 %collective-permute-start.29 = (bf16[1,128,2048]{2,1,0:T(8,128)(2,1)}, bf16[1,128,2048]{2,1,0:T(8,128)(2,1)}, u32[]{:S(2)}, u32[]{:S(2)}) collective-permute-start(bf16[1,128,2048]{2,1,0:T(8,128)(2,1)} %get-tuple-element.72), channel_id=1, source_target_pairs={{0,1},{1,0},{2,3},{3,2},{4,5},{5,4},{6,7},{7,6},{8,9},{9,8},{10,11... | collective-permute-start | bytes 1572872 | tf_op jit(solution)/shard_map/ppermute | solution.py:425
  157.4 17.7 %collective-permute-start.32 = (bf16[1,128,2048]{2,1,0:T(8,128)(2,1)}, bf16[1,128,2048]{2,1,0:T(8,128)(2,1)}, u32[]{:S(2)}, u32[]{:S(2)}) collective-permute-start(bf16[1,128,2048]{2,1,0:T(8,128)(2,1)} %get-tuple-element.74), channel_id=1, source_target_pairs={{0,1},{1,0},{2,3},{3,2},{4,5},{5,4},{6,7},{7,6},{8,9},{9,8},{10,11... | collective-permute-start | bytes 1572872 | tf_op jit(solution)/shard_map/ppermute | solution.py:425
  159.7 19.0 %collective-permute-start.13 = (bf16[128,2048]{1,0:T(8,128)(2,1)}, bf16[128,2048]{1,0:T(8,128)(2,1)}, u32[]{:S(2)}, u32[]{:S(2)}) collective-permute-start(bf16[128,2048]{1,0:T(8,128)(2,1)} %get-tuple-element.58), channel_id=1, source_target_pairs={{0,2},{1,3},{6,4},{7,5},{10,8},{11,9},{12,14},{13,15},{20,22},{21,... | collective-permute-start | bytes 1572872 | tf_op jit(solution)/shard_map/ppermute | solution.py:434
  166.9 23.1 %collective-permute-start.14 = (bf16[128,2048]{1,0:T(8,128)(2,1)}, bf16[128,2048]{1,0:T(8,128)(2,1)}, u32[]{:S(2)}, u32[]{:S(2)}) collective-permute-start(bf16[128,2048]{1,0:T(8,128)(2,1)} %get-tuple-element.59.refs_7_), channel_id=1, source_target_pairs={{6,2},{7,3},{0,4},{1,5},{12,8},{13,9},{10,14},{11,15},{18,22},{19,... | collective-permute-start | bytes 1572872 | tf_op jit(solution)/shard_map/ppermute | solution.py:434
  173.1 4.8 %copy-start.28 = (bf16[128,2048]{1,0:T(8,128)(2,1)}, bf16[128,2048]{1,0:T(8,128)(2,1)S(1)}, u32[]{:S(2)}) copy-start(bf16[128,2048]{1,0:T(8,128)(2,1)S(1)} %get-tuple-element.65.refs_6_) | copy-start | bytes 1572868
  173.1 24.4 %collective-permute-start.15 = (bf16[128,2048]{1,0:T(8,128)(2,1)}, bf16[128,2048]{1,0:T(8,128)(2,1)S(1)}, u32[]{:S(2)}, u32[]{:S(2)}) collective-permute-start(bf16[128,2048]{1,0:T(8,128)(2,1)} %get-tuple-element.58), channel_id=1, source_target_pairs={{4,2},{5,3},{2,4},{3,5},{14,8},{15,9},{8,14},{9,15},{16,22},{17,23... | collective-permute-start | bytes 1572872 | tf_op jit(solution)/shard_map/ppermute | solution.py:434
  173.8 25.2 %collective-permute-start.20 = (bf16[128,2048]{1,0:T(8,128)(2,1)S(1)}, bf16[128,2048]{1,0:T(8,128)(2,1)S(1)}, u32[]{:S(2)}, u32[]{:S(2)}) collective-permute-start(bf16[128,2048]{1,0:T(8,128)(2,1)S(1)} %get-tuple-element.64), channel_id=1, source_target_pairs={{2,0},{3,1},{4,6},{5,7},{8,10},{9,11},{14,12},{15,13},{22,20},{23,... | collective-permute-start | bytes 1572872 | tf_op jit(solution)/shard_map/ppermute | solution.py:438
  175.2 56.8 %collective-permute-start.21 = (bf16[128,2048]{1,0:T(8,128)(2,1)S(1)}, bf16[128,2048]{1,0:T(8,128)(2,1)S(1)}, u32[]{:S(2)}, u32[]{:S(2)}) collective-permute-start(bf16[128,2048]{1,0:T(8,128)(2,1)S(1)} %get-tuple-element.65.refs_6_), channel_id=1, source_target_pairs={{4,0},{5,1},{2,6},{3,7},{14,10},{15,11},{8,12},{9,13},{16,20},{17,... | collective-permute-start | bytes 1572872 | tf_op jit(solution)/shard_map/ppermute | solution.py:438
  176.5 19.0 %copy-start.23 = (f32[1,128,2048]{2,1,0:T(8,128)S(1)}, f32[1,128,2048]{2,1,0:T(8,128)}, u32[]{:S(2)}) copy-start(f32[1,128,2048]{2,1,0:T(8,128)} %copy-done.22) | copy-start | bytes 3145732
  176.5 19.0 %copy-start.25 = (f32[1,128,2048]{2,1,0:T(8,128)S(1)}, f32[1,128,2048]{2,1,0:T(8,128)}, u32[]{:S(2)}) copy-start(f32[1,128,2048]{2,1,0:T(8,128)} %copy-done.24) | copy-start | bytes 3145732
  178.7 55.4 %collective-permute-start.22 = (bf16[128,2048]{1,0:T(8,128)(2,1)S(1)}, bf16[128,2048]{1,0:T(8,128)(2,1)S(1)}, u32[]{:S(2)}, u32[]{:S(2)}) collective-permute-start(bf16[128,2048]{1,0:T(8,128)(2,1)S(1)} %get-tuple-element.64), channel_id=1, source_target_pairs={{6,0},{7,1},{0,6},{1,7},{12,10},{13,11},{10,12},{11,13},{18,20},{1... | collective-permute-start | bytes 1572872 | tf_op jit(solution)/shard_map/ppermute | solution.py:438
  190.0 46.2 %collective-permute-start.26 = (bf16[128,2048]{1,0:T(8,128)(2,1)}, bf16[128,2048]{1,0:T(8,128)(2,1)S(1)}, u32[]{:S(2)}, u32[]{:S(2)}) collective-permute-start(bf16[128,2048]{1,0:T(8,128)(2,1)} %get-tuple-element.69), channel_id=1, source_target_pairs={{0,2},{1,3},{6,4},{7,5},{10,8},{11,9},{12,14},{13,15},{20,22},{21,... | collective-permute-start | bytes 1572872 | tf_op jit(solution)/shard_map/ppermute | solution.py:434
  198.4 50.5 %collective-permute-start.28 = (bf16[128,2048]{1,0:T(8,128)(2,1)}, bf16[128,2048]{1,0:T(8,128)(2,1)S(1)}, u32[]{:S(2)}, u32[]{:S(2)}) collective-permute-start(bf16[128,2048]{1,0:T(8,128)(2,1)} %get-tuple-element.69), channel_id=1, source_target_pairs={{4,2},{5,3},{2,4},{3,5},{14,8},{15,9},{8,14},{9,15},{16,22},{17,23... | collective-permute-start | bytes 1572872 | tf_op jit(solution)/shard_map/ppermute | solution.py:434
  199.9 49.0 %collective-permute-start.27 = (bf16[128,2048]{1,0:T(8,128)(2,1)}, bf16[128,2048]{1,0:T(8,128)(2,1)S(1)}, u32[]{:S(2)}, u32[]{:S(2)}) collective-permute-start(bf16[128,2048]{1,0:T(8,128)(2,1)} %get-tuple-element.70.refs_8_), channel_id=1, source_target_pairs={{6,2},{7,3},{0,4},{1,5},{12,8},{13,9},{10,14},{11,15},{18,22},{19,... | collective-permute-start | bytes 1572872 | tf_op jit(solution)/shard_map/ppermute | solution.py:434
  232.8 37.1 %collective-permute-start.33 = (bf16[128,2048]{1,0:T(8,128)(2,1)}, bf16[128,2048]{1,0:T(8,128)(2,1)S(1)}, u32[]{:S(2)}, u32[]{:S(2)}) collective-permute-start(bf16[128,2048]{1,0:T(8,128)(2,1)} %get-tuple-element.75), channel_id=1, source_target_pairs={{2,0},{3,1},{4,6},{5,7},{8,10},{9,11},{14,12},{15,13},{22,20},{23,... | collective-permute-start | bytes 1572872 | tf_op jit(solution)/shard_map/ppermute | solution.py:438
  234.9 35.0 %collective-permute-start.34 = (bf16[128,2048]{1,0:T(8,128)(2,1)S(1)}, bf16[128,2048]{1,0:T(8,128)(2,1)S(1)}, u32[]{:S(2)}, u32[]{:S(2)}) collective-permute-start(bf16[128,2048]{1,0:T(8,128)(2,1)S(1)} %get-tuple-element.76.refs_7_), channel_id=1, source_target_pairs={{4,0},{5,1},{2,6},{3,7},{14,10},{15,11},{8,12},{9,13},{16,20},{17,... | collective-permute-start | bytes 1572872 | tf_op jit(solution)/shard_map/ppermute | solution.py:438
  236.2 33.7 %collective-permute-start.35 = (bf16[128,2048]{1,0:T(8,128)(2,1)}, bf16[128,2048]{1,0:T(8,128)(2,1)}, u32[]{:S(2)}, u32[]{:S(2)}) collective-permute-start(bf16[128,2048]{1,0:T(8,128)(2,1)} %get-tuple-element.75), channel_id=1, source_target_pairs={{6,0},{7,1},{0,6},{1,7},{12,10},{13,11},{10,12},{11,13},{18,20},{1... | collective-permute-start | bytes 1572872 | tf_op jit(solution)/shard_map/ppermute | solution.py:438
  (29 other events, 33.2 us)
